TPU v7x, 128 devices: a whole 4x4x4 slice. The times are simulated.
128 devices in a mesh: gx: 8 (over y, core), gy: 16 (over x, z).
Axes of the slice: x: 4, y: 4, z: 4, core: 2. Of those that a mesh axis runs over, the one named last changes fastest.
Arguments:
- points: bfloat16 [524288, 128], P(('gx', 'gy')), may hold values from -6 to 6
- occupied: int32 [524288], P(('gx', 'gy')), may hold values 0 or 1
- z_order: int32 [128, 4096], P(('gx', 'gy')), may hold values from 0 to 4095, each once within a row
- pad_mask: int32 [128, 4096], P(('gx', 'gy')), may hold values 0 or 1
- hilbert_order: int32 [128, 4096], P(('gx', 'gy')), may hold values from 0 to 4095, each once within a row
- send_counts: int32 [128, 128], P(('gx', 'gy')), may hold values from 0 to 40, as said below
- w_conv: bfloat16 [27, 128, 128], replicated, may hold values from -0.109375 to 0.109375
- cpe_proj: bfloat16 [128, 128], replicated, may hold values from -0.5 to 0.5
- cpe_gain: float32 [128], replicated, may hold values from 0.5 to 1.5
- attn_gain: float32 [128], replicated, may hold values from 0.5 to 1.5
- w_qkv: bfloat16 [128, 384], replicated, may hold values from -4 to 4
- w_out: bfloat16 [128, 128], replicated, may hold values from -0.5 to 0.5
- mlp_gain: float32 [128], replicated, may hold values from 0.5 to 1.5
- w_up: bfloat16 [128, 512], replicated, may hold values from -0.5 to 0.5
- w_down: bfloat16 [512, 128], replicated, may hold values from -0.25 to 0.25
Outputs:
- moved: bfloat16 [655360, 128], P(('gx', 'gy'))
Inputs may be any that keep to these rules, and one draw needn't show every extreme that they name: `send_counts`: each row sums to 4096; one new owner receives exactly 40 rows from every tile.
All inputs are finite; a program needn't handle non-finite values. No bound on the sum of `occupied` or of `pad_mask` on one device may be relied on, other than what follows from the above.
Results may differ from a plain program's by a relative error of at most 0.012.
The roundings to bfloat16 on the way count: a program that leaves them out, or rounds other values in their place, can miss the bound.
Values may be sent and summed in bfloat16 or wider, within the bound.
A program may use at most 64 MiB of HBM per device.

v0:
```python
import jax
import jax.numpy as jnp
from jax import lax
from jax.sharding import PartitionSpec as P

C = 128
HEADS = 8
PATCH = 1024
LA = 16
LB = 16
HEAD_DIM = 16


def padded(x, sides, width):
    for axis, dim in sides:
        devices, length = (lax.axis_size(axis), x.shape[dim])
        up = [(i, (i + 1) % devices) for i in range(devices - 1)]
        down = [(j, i) for i, j in up]
        last = lax.slice_in_dim(x, length - width, length, axis=dim)
        initial = lax.slice_in_dim(x, 0, width, axis=dim)
        before = lax.ppermute(last, axis, up)
        after = lax.ppermute(initial, axis, down)
        x = jnp.concatenate([before, x, after], axis=dim)
    return x


def layer_norm(values, gain):
    center = values - jnp.mean(values, axis=-1, keepdims=True)
    spread = jnp.mean(center * center, axis=-1, keepdims=True)
    return center * lax.rsqrt(spread + 1e-05) * gain


def attend(block_items):
    queries, keys_in, values_in, alive_keys = block_items
    scores = jnp.einsum(
        "hqd,hkd->hqk", queries, keys_in, preferred_element_type=jnp.float32
    ) * HEAD_DIM ** (-0.5)
    length = scores.shape[-1]
    diagonal_mask = lax.broadcasted_iota(jnp.int32, (1, length, length), 1) == lax.broadcasted_iota(
        jnp.int32, (1, length, length), 2
    )
    allowed = (alive_keys[None, None, :] > 0) | diagonal_mask
    masked = jnp.where(allowed, scores, -1e30)
    row_peak = jnp.max(masked, axis=-1, keepdims=True)
    weights = jnp.where(allowed, jnp.exp(masked - row_peak), 0.0)
    attn_probs = (weights / jnp.sum(weights, axis=-1, keepdims=True)).astype(jnp.bfloat16)
    mixed_heads = jnp.einsum(
        "hqk,hkd->hqd", attn_probs, values_in, preferred_element_type=jnp.float32
    )
    return mixed_heads.astype(jnp.bfloat16)


def split_heads(matrix, patch_count):
    shaped = matrix.reshape(patch_count, PATCH, HEADS // 2, 2, HEAD_DIM).transpose(0, 2, 3, 1, 4)
    return shaped.reshape(patch_count * (HEADS // 2), 2, PATCH, HEAD_DIM)


def join_heads(blocks, patch_count):
    shaped = blocks.reshape(patch_count, HEADS // 2, 2, PATCH, HEAD_DIM).transpose(0, 3, 1, 2, 4)
    return shaped.reshape(patch_count * PATCH, C)


def body(
    points,
    occupied,
    z_order,
    pad_mask,
    hilbert_order,
    send_counts,
    w_conv,
    cpe_proj,
    cpe_gain,
    attn_gain,
    w_qkv,
    w_out,
    mlp_gain,
    w_up,
    w_down,
):
    point_count, width = points.shape
    depth = point_count // (LA * LB)
    filled = jnp.where(occupied[:, None] > 0, points, jnp.zeros_like(points))
    voxels = filled.reshape(LA, LB, depth, width)
    window = padded(voxels, (("gx", 0), ("gy", 1)), 1)
    window = jnp.pad(window, ((0, 0), (0, 0), (1, 1), (0, 0)))
    conv_sum = jnp.zeros((point_count, width), jnp.float32)
    for step_a in range(3):
        for step_b in range(3):
            for step_z in range(3):
                tap = step_a * 9 + step_b * 3 + step_z
                piece = window[
                    step_a : step_a + LA, step_b : step_b + LB, step_z : step_z + depth
                ].reshape(point_count, width)
                conv_sum = conv_sum + jnp.dot(
                    piece, w_conv[tap], preferred_element_type=jnp.float32
                )
    conv_out = conv_sum.astype(jnp.bfloat16)
    encoded = layer_norm(jnp.dot(conv_out, cpe_proj, preferred_element_type=jnp.float32), cpe_gain)
    residual = points.astype(jnp.float32) + encoded
    serial = jnp.take(residual, z_order[0], axis=0)
    attn_in = layer_norm(serial, attn_gain).astype(jnp.bfloat16)
    projected = jnp.dot(attn_in, w_qkv, preferred_element_type=jnp.float32).astype(jnp.bfloat16)
    patch_count = point_count // PATCH
    alive_row = pad_mask[0]
    queries = split_heads(projected[:, :width], patch_count)
    keys_in = split_heads(projected[:, width : 2 * width], patch_count)
    values_in = split_heads(projected[:, 2 * width :], patch_count)
    alive_keys = jnp.broadcast_to(
        alive_row.reshape(patch_count, 1, PATCH), (patch_count, HEADS // 2, PATCH)
    ).reshape(-1, PATCH)
    heads_out = join_heads(lax.map(attend, (queries, keys_in, values_in, alive_keys)), patch_count)
    attn_part = jnp.dot(heads_out, w_out, preferred_element_type=jnp.float32)
    mixed = serial + alive_row.astype(jnp.float32)[:, None] * attn_part
    mlp_in = layer_norm(mixed, mlp_gain).astype(jnp.bfloat16)
    hidden = jax.nn.gelu(jnp.dot(mlp_in, w_up, preferred_element_type=jnp.float32)).astype(
        jnp.bfloat16
    )
    block_out = (mixed + jnp.dot(hidden, w_down, preferred_element_type=jnp.float32)).astype(
        jnp.bfloat16
    )
    device_total = lax.axis_size("gx") * lax.axis_size("gy")
    capacity = point_count // device_total + max(2, point_count // (4 * device_total))
    count_row = send_counts[0]
    starts = jnp.cumsum(count_row) - count_row
    slot_ids = jnp.arange(capacity, dtype=jnp.int32)
    picks = jnp.clip(starts[:, None] + slot_ids[None, :], 0, point_count - 1).reshape(-1)
    valid = slot_ids[None, :] < count_row[:, None]
    source_rows = jnp.take(hilbert_order[0], picks, axis=0)
    rows_out = jnp.take(block_out, source_rows, axis=0).reshape(device_total, capacity, width)
    send_buffer = jnp.where(valid[:, :, None], rows_out, jnp.zeros_like(rows_out))
    received = lax.all_to_all(send_buffer, ("gx", "gy"), split_axis=0, concat_axis=0, tiled=True)
    return received.reshape(device_total * capacity, width)


def solution(mesh):
    placed = (
        P(("gx", "gy"), None),
        P(("gx", "gy")),
        P(("gx", "gy"), None),
        P(("gx", "gy"), None),
        P(("gx", "gy"), None),
        P(("gx", "gy"), None),
        P(),
        P(),
        P(),
        P(),
        P(),
        P(),
        P(),
        P(),
        P(),
    )
    return jax.shard_map(
        body, mesh=mesh, in_specs=placed, out_specs=P(("gx", "gy"), None), check_vma=False
    )
```

profile of v0, /device:TPU:1, one launch (start us, length us, event | category | flops | bytes accessed | tf_op | source)
XLA Modules:
  0.0 404.3 jit_solution(12771679014486402992)
XLA Ops:
  0.8 3.4 broadcast_select_fusion
  4.2 4.6 %collective-permute-start = (bf16[1,16,16,128]{3,2,1,0:T(8,128)(2,1)S(1)}, bf16[1,16,16,128]{3,2,1,0:T(8,128)(2,1)S(1)}, u32[]{:S(2)}, u32[]{:S(2)}) collective-permute-start(bf16[1,16,16,128]{3,2,1,0:T(8,128)(2,1)S(1)} %bitcast.267), channel_id=1, source_target_pairs={{0,16},{16,32},{32,48},{48,64},{64,80},{80,96},{96,112},{1,17},{17... | collective-permute-start | bytes 196616 | tf_op jit(solution)/shard_map/ppermute | solution.py:21
  11.5 28.7 %gather_fusion = s32[5120]{0:T(1024)S(1)} fusion(s32[4096]{0:T(1024)S(1)} %bitcast.218, s32[5120]{0:T(1024)S(1)} %broadcast_clamp_fusion.1), kind=kCustom, calls=%fused_computation | custom fusion | bytes 61440 | tf_op jit(solution)/shard_map/jit(_take)/gather | solution.py:128
  44.3 3.5 collective-permute-start.2
  50.3 2.9 collective-permute-done.3
  54.9 6.5 %fusion.145 = (bf16[16,16,16,128]{3,2,1,0:T(8,128)(2,1)}, bf16[16,16,16,128]{3,2,1,0:T(8,128)(2,1)S(1)}, bf16[16,16,16,128]{3,2,1,0:T(8,128)(2,1)}, bf16[16,16,1...) fusion(bf16[18,18,18,128]{3,2,1,0:T(8,128)(2,1)S(1)} %select_ma, ...), kind=kLoop, calls=%fused_computation.197 | loop fusion | bytes 37748736 | tf_op jit(solution)/shard_map/slice | solution.py:91
  84.1 2.5 fusion.150
  91.5 14.2 %gather_fusion.1 = f32[4096,128]{1,0:T(8,128)} fusion(f32[4096,128]{1,0:T(8,128)S(1)} %copy.40, s32[4096]{0:T(1024)S(1)} %broadcast_clamp_fusion.2), kind=kCustom, calls=%fused_computation.1 | custom fusion | bytes 4210688 | tf_op jit(solution)/shard_map/jit(_take)/gather | solution.py:100
  105.7 2.1 copy.41
  114.8 2.6 copy.43
  120.5 2.5 copy.45
  126.1 2.5 copy.47
  128.6 213.3 %while.10 = (s32[]{:T(128)}, bf16[16,2,1024,16]{2,3,1,0:T(8,128)(2,1)}, s32[16,1024]{1,0:T(8,128)S(1)}, bf16[16,2,1024,16]{2,3,1,0:T(8,128)(2,1)}, bf16[16,2,102...) while((s32[]{:T(128)}, bf16[16,2,1024,16]{2,3,1,0:T(8,128)(2,1)}, ...), condition=%wide.region_8.9_spmd, body=%wide.region_5.8_spmd.sunk | while | flops 151029760 | bytes 20209744 | solution.py:111
  129.0 8.2 %fusion.197 = (f32[2,1024]{1,0:T(2,128)S(1)}, f32[2,1024,1024]{1,2,0:T(8,128)}) fusion(pred[1024,1024]{0,1:T(8,128)(4,1)S(1)} %fusion.196, bf16[16,2,1024,16]{2,3,1,0:T(8,128)(2,1)} %get-tuple-element.157, s32[]{:T(128)} %get-tuple-element.146, bf16[16,2,1024,16]{2,3,1,0:T(8,128)(2,1)} %get-tuple-element.156), kind=kOutput, calls=%fused_computation.195.clone.1 | convolution fusion | flops 77595648 | bytes 10626048 | tf_op jit(solution)/shard_map/while/body/eval_jaxpr/sub | solution.py:45
  137.2 4.7 %fusion.198 = bf16[16,2,1024,16]{2,3,1,0:T(8,128)(2,1)} fusion(bf16[16,2,1024,16]{2,3,1,0:T(8,128)(2,1)} %get-tuple-element.147, s32[]{:T(128)} %get-tuple-element.146, f32[2,1024,1024]{1,2,0:T(8,128)} %get-tuple-element.137, f32[2,1024]{1,0:T(2,128)S(1)} %get-tuple-element.138, bf16[16,2,1024,16]{2,3,1,0:T(8,128)(2,1)} %get-tuple-element.158), kind=kOutput, calls=%fused_computation.16.clone.1 | convolution fusion | flops 71335936 | bytes 8528896 | tf_op jit(solution)/shard_map/while/body/eval_jaxpr/hqk,hkd->hqd/dot_general | solution.py:47
  142.3 8.2 %fusion.197 = (f32[2,1024]{1,0:T(2,128)S(1)}, f32[2,1024,1024]{1,2,0:T(8,128)}) fusion(pred[1024,1024]{0,1:T(8,128)(4,1)S(1)} %fusion.196, bf16[16,2,1024,16]{2,3,1,0:T(8,128)(2,1)} %get-tuple-element.157, s32[]{:T(128)} %get-tuple-element.146, bf16[16,2,1024,16]{2,3,1,0:T(8,128)(2,1)} %get-tuple-element.156), kind=kOutput, calls=%fused_computation.195.clone.1 | convolution fusion | flops 77595648 | bytes 10626048 | tf_op jit(solution)/shard_map/while/body/eval_jaxpr/sub | solution.py:45
  150.5 4.7 %fusion.198 = bf16[16,2,1024,16]{2,3,1,0:T(8,128)(2,1)} fusion(bf16[16,2,1024,16]{2,3,1,0:T(8,128)(2,1)} %get-tuple-element.147, s32[]{:T(128)} %get-tuple-element.146, f32[2,1024,1024]{1,2,0:T(8,128)} %get-tuple-element.137, f32[2,1024]{1,0:T(2,128)S(1)} %get-tuple-element.138, bf16[16,2,1024,16]{2,3,1,0:T(8,128)(2,1)} %get-tuple-element.158), kind=kOutput, calls=%fused_computation.16.clone.1 | convolution fusion | flops 71335936 | bytes 8528896 | tf_op jit(solution)/shard_map/while/body/eval_jaxpr/hqk,hkd->hqd/dot_general | solution.py:47
  155.6 8.2 %fusion.197 = (f32[2,1024]{1,0:T(2,128)S(1)}, f32[2,1024,1024]{1,2,0:T(8,128)}) fusion(pred[1024,1024]{0,1:T(8,128)(4,1)S(1)} %fusion.196, bf16[16,2,1024,16]{2,3,1,0:T(8,128)(2,1)} %get-tuple-element.157, s32[]{:T(128)} %get-tuple-element.146, bf16[16,2,1024,16]{2,3,1,0:T(8,128)(2,1)} %get-tuple-element.156), kind=kOutput, calls=%fused_computation.195.clone.1 | convolution fusion | flops 77595648 | bytes 10626048 | tf_op jit(solution)/shard_map/while/body/eval_jaxpr/sub | solution.py:45
  163.9 4.7 %fusion.198 = bf16[16,2,1024,16]{2,3,1,0:T(8,128)(2,1)} fusion(bf16[16,2,1024,16]{2,3,1,0:T(8,128)(2,1)} %get-tuple-element.147, s32[]{:T(128)} %get-tuple-element.146, f32[2,1024,1024]{1,2,0:T(8,128)} %get-tuple-element.137, f32[2,1024]{1,0:T(2,128)S(1)} %get-tuple-element.138, bf16[16,2,1024,16]{2,3,1,0:T(8,128)(2,1)} %get-tuple-element.158), kind=kOutput, calls=%fused_computation.16.clone.1 | convolution fusion | flops 71335936 | bytes 8528896 | tf_op jit(solution)/shard_map/while/body/eval_jaxpr/hqk,hkd->hqd/dot_general | solution.py:47
  169.0 8.2 %fusion.197 = (f32[2,1024]{1,0:T(2,128)S(1)}, f32[2,1024,1024]{1,2,0:T(8,128)}) fusion(pred[1024,1024]{0,1:T(8,128)(4,1)S(1)} %fusion.196, bf16[16,2,1024,16]{2,3,1,0:T(8,128)(2,1)} %get-tuple-element.157, s32[]{:T(128)} %get-tuple-element.146, bf16[16,2,1024,16]{2,3,1,0:T(8,128)(2,1)} %get-tuple-element.156), kind=kOutput, calls=%fused_computation.195.clone.1 | convolution fusion | flops 77595648 | bytes 10626048 | tf_op jit(solution)/shard_map/while/body/eval_jaxpr/sub | solution.py:45
  177.2 4.7 %fusion.198 = bf16[16,2,1024,16]{2,3,1,0:T(8,128)(2,1)} fusion(bf16[16,2,1024,16]{2,3,1,0:T(8,128)(2,1)} %get-tuple-element.147, s32[]{:T(128)} %get-tuple-element.146, f32[2,1024,1024]{1,2,0:T(8,128)} %get-tuple-element.137, f32[2,1024]{1,0:T(2,128)S(1)} %get-tuple-element.138, bf16[16,2,1024,16]{2,3,1,0:T(8,128)(2,1)} %get-tuple-element.158), kind=kOutput, calls=%fused_computation.16.clone.1 | convolution fusion | flops 71335936 | bytes 8528896 | tf_op jit(solution)/shard_map/while/body/eval_jaxpr/hqk,hkd->hqd/dot_general | solution.py:47
  182.3 8.2 %fusion.197 = (f32[2,1024]{1,0:T(2,128)S(1)}, f32[2,1024,1024]{1,2,0:T(8,128)}) fusion(pred[1024,1024]{0,1:T(8,128)(4,1)S(1)} %fusion.196, bf16[16,2,1024,16]{2,3,1,0:T(8,128)(2,1)} %get-tuple-element.157, s32[]{:T(128)} %get-tuple-element.146, bf16[16,2,1024,16]{2,3,1,0:T(8,128)(2,1)} %get-tuple-element.156), kind=kOutput, calls=%fused_computation.195.clone.1 | convolution fusion | flops 77595648 | bytes 10626048 | tf_op jit(solution)/shard_map/while/body/eval_jaxpr/sub | solution.py:45
  190.5 4.7 %fusion.198 = bf16[16,2,1024,16]{2,3,1,0:T(8,128)(2,1)} fusion(bf16[16,2,1024,16]{2,3,1,0:T(8,128)(2,1)} %get-tuple-element.147, s32[]{:T(128)} %get-tuple-element.146, f32[2,1024,1024]{1,2,0:T(8,128)} %get-tuple-element.137, f32[2,1024]{1,0:T(2,128)S(1)} %get-tuple-element.138, bf16[16,2,1024,16]{2,3,1,0:T(8,128)(2,1)} %get-tuple-element.158), kind=kOutput, calls=%fused_computation.16.clone.1 | convolution fusion | flops 71335936 | bytes 8528896 | tf_op jit(solution)/shard_map/while/body/eval_jaxpr/hqk,hkd->hqd/dot_general | solution.py:47
  195.6 8.2 %fusion.197 = (f32[2,1024]{1,0:T(2,128)S(1)}, f32[2,1024,1024]{1,2,0:T(8,128)}) fusion(pred[1024,1024]{0,1:T(8,128)(4,1)S(1)} %fusion.196, bf16[16,2,1024,16]{2,3,1,0:T(8,128)(2,1)} %get-tuple-element.157, s32[]{:T(128)} %get-tuple-element.146, bf16[16,2,1024,16]{2,3,1,0:T(8,128)(2,1)} %get-tuple-element.156), kind=kOutput, calls=%fused_computation.195.clone.1 | convolution fusion | flops 77595648 | bytes 10626048 | tf_op jit(solution)/shard_map/while/body/eval_jaxpr/sub | solution.py:45
  203.9 4.7 %fusion.198 = bf16[16,2,1024,16]{2,3,1,0:T(8,128)(2,1)} fusion(bf16[16,2,1024,16]{2,3,1,0:T(8,128)(2,1)} %get-tuple-element.147, s32[]{:T(128)} %get-tuple-element.146, f32[2,1024,1024]{1,2,0:T(8,128)} %get-tuple-element.137, f32[2,1024]{1,0:T(2,128)S(1)} %get-tuple-element.138, bf16[16,2,1024,16]{2,3,1,0:T(8,128)(2,1)} %get-tuple-element.158), kind=kOutput, calls=%fused_computation.16.clone.1 | convolution fusion | flops 71335936 | bytes 8528896 | tf_op jit(solution)/shard_map/while/body/eval_jaxpr/hqk,hkd->hqd/dot_general | solution.py:47
  209.0 8.2 %fusion.197 = (f32[2,1024]{1,0:T(2,128)S(1)}, f32[2,1024,1024]{1,2,0:T(8,128)}) fusion(pred[1024,1024]{0,1:T(8,128)(4,1)S(1)} %fusion.196, bf16[16,2,1024,16]{2,3,1,0:T(8,128)(2,1)} %get-tuple-element.157, s32[]{:T(128)} %get-tuple-element.146, bf16[16,2,1024,16]{2,3,1,0:T(8,128)(2,1)} %get-tuple-element.156), kind=kOutput, calls=%fused_computation.195.clone.1 | convolution fusion | flops 77595648 | bytes 10626048 | tf_op jit(solution)/shard_map/while/body/eval_jaxpr/sub | solution.py:45
  217.2 4.7 %fusion.198 = bf16[16,2,1024,16]{2,3,1,0:T(8,128)(2,1)} fusion(bf16[16,2,1024,16]{2,3,1,0:T(8,128)(2,1)} %get-tuple-element.147, s32[]{:T(128)} %get-tuple-element.146, f32[2,1024,1024]{1,2,0:T(8,128)} %get-tuple-element.137, f32[2,1024]{1,0:T(2,128)S(1)} %get-tuple-element.138, bf16[16,2,1024,16]{2,3,1,0:T(8,128)(2,1)} %get-tuple-element.158), kind=kOutput, calls=%fused_computation.16.clone.1 | convolution fusion | flops 71335936 | bytes 8528896 | tf_op jit(solution)/shard_map/while/body/eval_jaxpr/hqk,hkd->hqd/dot_general | solution.py:47
  222.3 8.2 %fusion.197 = (f32[2,1024]{1,0:T(2,128)S(1)}, f32[2,1024,1024]{1,2,0:T(8,128)}) fusion(pred[1024,1024]{0,1:T(8,128)(4,1)S(1)} %fusion.196, bf16[16,2,1024,16]{2,3,1,0:T(8,128)(2,1)} %get-tuple-element.157, s32[]{:T(128)} %get-tuple-element.146, bf16[16,2,1024,16]{2,3,1,0:T(8,128)(2,1)} %get-tuple-element.156), kind=kOutput, calls=%fused_computation.195.clone.1 | convolution fusion | flops 77595648 | bytes 10626048 | tf_op jit(solution)/shard_map/while/body/eval_jaxpr/sub | solution.py:45
  230.5 4.7 %fusion.198 = bf16[16,2,1024,16]{2,3,1,0:T(8,128)(2,1)} fusion(bf16[16,2,1024,16]{2,3,1,0:T(8,128)(2,1)} %get-tuple-element.147, s32[]{:T(128)} %get-tuple-element.146, f32[2,1024,1024]{1,2,0:T(8,128)} %get-tuple-element.137, f32[2,1024]{1,0:T(2,128)S(1)} %get-tuple-element.138, bf16[16,2,1024,16]{2,3,1,0:T(8,128)(2,1)} %get-tuple-element.158), kind=kOutput, calls=%fused_computation.16.clone.1 | convolution fusion | flops 71335936 | bytes 8528896 | tf_op jit(solution)/shard_map/while/body/eval_jaxpr/hqk,hkd->hqd/dot_general | solution.py:47
  235.6 8.2 %fusion.197 = (f32[2,1024]{1,0:T(2,128)S(1)}, f32[2,1024,1024]{1,2,0:T(8,128)}) fusion(pred[1024,1024]{0,1:T(8,128)(4,1)S(1)} %fusion.196, bf16[16,2,1024,16]{2,3,1,0:T(8,128)(2,1)} %get-tuple-element.157, s32[]{:T(128)} %get-tuple-element.146, bf16[16,2,1024,16]{2,3,1,0:T(8,128)(2,1)} %get-tuple-element.156), kind=kOutput, calls=%fused_computation.195.clone.1 | convolution fusion | flops 77595648 | bytes 10626048 | tf_op jit(solution)/shard_map/while/body/eval_jaxpr/sub | solution.py:45
  243.8 4.7 %fusion.198 = bf16[16,2,1024,16]{2,3,1,0:T(8,128)(2,1)} fusion(bf16[16,2,1024,16]{2,3,1,0:T(8,128)(2,1)} %get-tuple-element.147, s32[]{:T(128)} %get-tuple-element.146, f32[2,1024,1024]{1,2,0:T(8,128)} %get-tuple-element.137, f32[2,1024]{1,0:T(2,128)S(1)} %get-tuple-element.138, bf16[16,2,1024,16]{2,3,1,0:T(8,128)(2,1)} %get-tuple-element.158), kind=kOutput, calls=%fused_computation.16.clone.1 | convolution fusion | flops 71335936 | bytes 8528896 | tf_op jit(solution)/shard_map/while/body/eval_jaxpr/hqk,hkd->hqd/dot_general | solution.py:47
  248.9 8.2 %fusion.197 = (f32[2,1024]{1,0:T(2,128)S(1)}, f32[2,1024,1024]{1,2,0:T(8,128)}) fusion(pred[1024,1024]{0,1:T(8,128)(4,1)S(1)} %fusion.196, bf16[16,2,1024,16]{2,3,1,0:T(8,128)(2,1)} %get-tuple-element.157, s32[]{:T(128)} %get-tuple-element.146, bf16[16,2,1024,16]{2,3,1,0:T(8,128)(2,1)} %get-tuple-element.156), kind=kOutput, calls=%fused_computation.195.clone.1 | convolution fusion | flops 77595648 | bytes 10626048 | tf_op jit(solution)/shard_map/while/body/eval_jaxpr/sub | solution.py:45
  257.2 4.7 %fusion.198 = bf16[16,2,1024,16]{2,3,1,0:T(8,128)(2,1)} fusion(bf16[16,2,1024,16]{2,3,1,0:T(8,128)(2,1)} %get-tuple-element.147, s32[]{:T(128)} %get-tuple-element.146, f32[2,1024,1024]{1,2,0:T(8,128)} %get-tuple-element.137, f32[2,1024]{1,0:T(2,128)S(1)} %get-tuple-element.138, bf16[16,2,1024,16]{2,3,1,0:T(8,128)(2,1)} %get-tuple-element.158), kind=kOutput, calls=%fused_computation.16.clone.1 | convolution fusion | flops 71335936 | bytes 8528896 | tf_op jit(solution)/shard_map/while/body/eval_jaxpr/hqk,hkd->hqd/dot_general | solution.py:47
  262.3 8.2 %fusion.197 = (f32[2,1024]{1,0:T(2,128)S(1)}, f32[2,1024,1024]{1,2,0:T(8,128)}) fusion(pred[1024,1024]{0,1:T(8,128)(4,1)S(1)} %fusion.196, bf16[16,2,1024,16]{2,3,1,0:T(8,128)(2,1)} %get-tuple-element.157, s32[]{:T(128)} %get-tuple-element.146, bf16[16,2,1024,16]{2,3,1,0:T(8,128)(2,1)} %get-tuple-element.156), kind=kOutput, calls=%fused_computation.195.clone.1 | convolution fusion | flops 77595648 | bytes 10626048 | tf_op jit(solution)/shard_map/while/body/eval_jaxpr/sub | solution.py:45
  270.5 4.7 %fusion.198 = bf16[16,2,1024,16]{2,3,1,0:T(8,128)(2,1)} fusion(bf16[16,2,1024,16]{2,3,1,0:T(8,128)(2,1)} %get-tuple-element.147, s32[]{:T(128)} %get-tuple-element.146, f32[2,1024,1024]{1,2,0:T(8,128)} %get-tuple-element.137, f32[2,1024]{1,0:T(2,128)S(1)} %get-tuple-element.138, bf16[16,2,1024,16]{2,3,1,0:T(8,128)(2,1)} %get-tuple-element.158), kind=kOutput, calls=%fused_computation.16.clone.1 | convolution fusion | flops 71335936 | bytes 8528896 | tf_op jit(solution)/shard_map/while/body/eval_jaxpr/hqk,hkd->hqd/dot_general | solution.py:47
  275.6 8.2 %fusion.197 = (f32[2,1024]{1,0:T(2,128)S(1)}, f32[2,1024,1024]{1,2,0:T(8,128)}) fusion(pred[1024,1024]{0,1:T(8,128)(4,1)S(1)} %fusion.196, bf16[16,2,1024,16]{2,3,1,0:T(8,128)(2,1)} %get-tuple-element.157, s32[]{:T(128)} %get-tuple-element.146, bf16[16,2,1024,16]{2,3,1,0:T(8,128)(2,1)} %get-tuple-element.156), kind=kOutput, calls=%fused_computation.195.clone.1 | convolution fusion | flops 77595648 | bytes 10626048 | tf_op jit(solution)/shard_map/while/body/eval_jaxpr/sub | solution.py:45
  283.8 4.7 %fusion.198 = bf16[16,2,1024,16]{2,3,1,0:T(8,128)(2,1)} fusion(bf16[16,2,1024,16]{2,3,1,0:T(8,128)(2,1)} %get-tuple-element.147, s32[]{:T(128)} %get-tuple-element.146, f32[2,1024,1024]{1,2,0:T(8,128)} %get-tuple-element.137, f32[2,1024]{1,0:T(2,128)S(1)} %get-tuple-element.138, bf16[16,2,1024,16]{2,3,1,0:T(8,128)(2,1)} %get-tuple-element.158), kind=kOutput, calls=%fused_computation.16.clone.1 | convolution fusion | flops 71335936 | bytes 8528896 | tf_op jit(solution)/shard_map/while/body/eval_jaxpr/hqk,hkd->hqd/dot_general | solution.py:47
  288.9 8.2 %fusion.197 = (f32[2,1024]{1,0:T(2,128)S(1)}, f32[2,1024,1024]{1,2,0:T(8,128)}) fusion(pred[1024,1024]{0,1:T(8,128)(4,1)S(1)} %fusion.196, bf16[16,2,1024,16]{2,3,1,0:T(8,128)(2,1)} %get-tuple-element.157, s32[]{:T(128)} %get-tuple-element.146, bf16[16,2,1024,16]{2,3,1,0:T(8,128)(2,1)} %get-tuple-element.156), kind=kOutput, calls=%fused_computation.195.clone.1 | convolution fusion | flops 77595648 | bytes 10626048 | tf_op jit(solution)/shard_map/while/body/eval_jaxpr/sub | solution.py:45
  297.2 4.7 %fusion.198 = bf16[16,2,1024,16]{2,3,1,0:T(8,128)(2,1)} fusion(bf16[16,2,1024,16]{2,3,1,0:T(8,128)(2,1)} %get-tuple-element.147, s32[]{:T(128)} %get-tuple-element.146, f32[2,1024,1024]{1,2,0:T(8,128)} %get-tuple-element.137, f32[2,1024]{1,0:T(2,128)S(1)} %get-tuple-element.138, bf16[16,2,1024,16]{2,3,1,0:T(8,128)(2,1)} %get-tuple-element.158), kind=kOutput, calls=%fused_computation.16.clone.1 | convolution fusion | flops 71335936 | bytes 8528896 | tf_op jit(solution)/shard_map/while/body/eval_jaxpr/hqk,hkd->hqd/dot_general | solution.py:47
  302.3 8.2 %fusion.197 = (f32[2,1024]{1,0:T(2,128)S(1)}, f32[2,1024,1024]{1,2,0:T(8,128)}) fusion(pred[1024,1024]{0,1:T(8,128)(4,1)S(1)} %fusion.196, bf16[16,2,1024,16]{2,3,1,0:T(8,128)(2,1)} %get-tuple-element.157, s32[]{:T(128)} %get-tuple-element.146, bf16[16,2,1024,16]{2,3,1,0:T(8,128)(2,1)} %get-tuple-element.156), kind=kOutput, calls=%fused_computation.195.clone.1 | convolution fusion | flops 77595648 | bytes 10626048 | tf_op jit(solution)/shard_map/while/body/eval_jaxpr/sub | solution.py:45
  310.5 4.7 %fusion.198 = bf16[16,2,1024,16]{2,3,1,0:T(8,128)(2,1)} fusion(bf16[16,2,1024,16]{2,3,1,0:T(8,128)(2,1)} %get-tuple-element.147, s32[]{:T(128)} %get-tuple-element.146, f32[2,1024,1024]{1,2,0:T(8,128)} %get-tuple-element.137, f32[2,1024]{1,0:T(2,128)S(1)} %get-tuple-element.138, bf16[16,2,1024,16]{2,3,1,0:T(8,128)(2,1)} %get-tuple-element.158), kind=kOutput, calls=%fused_computation.16.clone.1 | convolution fusion | flops 71335936 | bytes 8528896 | tf_op jit(solution)/shard_map/while/body/eval_jaxpr/hqk,hkd->hqd/dot_general | solution.py:47
  315.6 8.2 %fusion.197 = (f32[2,1024]{1,0:T(2,128)S(1)}, f32[2,1024,1024]{1,2,0:T(8,128)}) fusion(pred[1024,1024]{0,1:T(8,128)(4,1)S(1)} %fusion.196, bf16[16,2,1024,16]{2,3,1,0:T(8,128)(2,1)} %get-tuple-element.157, s32[]{:T(128)} %get-tuple-element.146, bf16[16,2,1024,16]{2,3,1,0:T(8,128)(2,1)} %get-tuple-element.156), kind=kOutput, calls=%fused_computation.195.clone.1 | convolution fusion | flops 77595648 | bytes 10626048 | tf_op jit(solution)/shard_map/while/body/eval_jaxpr/sub | solution.py:45
  323.8 4.7 %fusion.198 = bf16[16,2,1024,16]{2,3,1,0:T(8,128)(2,1)} fusion(bf16[16,2,1024,16]{2,3,1,0:T(8,128)(2,1)} %get-tuple-element.147, s32[]{:T(128)} %get-tuple-element.146, f32[2,1024,1024]{1,2,0:T(8,128)} %get-tuple-element.137, f32[2,1024]{1,0:T(2,128)S(1)} %get-tuple-element.138, bf16[16,2,1024,16]{2,3,1,0:T(8,128)(2,1)} %get-tuple-element.158), kind=kOutput, calls=%fused_computation.16.clone.1 | convolution fusion | flops 71335936 | bytes 8528896 | tf_op jit(solution)/shard_map/while/body/eval_jaxpr/hqk,hkd->hqd/dot_general | solution.py:47
  328.9 8.2 %fusion.197 = (f32[2,1024]{1,0:T(2,128)S(1)}, f32[2,1024,1024]{1,2,0:T(8,128)}) fusion(pred[1024,1024]{0,1:T(8,128)(4,1)S(1)} %fusion.196, bf16[16,2,1024,16]{2,3,1,0:T(8,128)(2,1)} %get-tuple-element.157, s32[]{:T(128)} %get-tuple-element.146, bf16[16,2,1024,16]{2,3,1,0:T(8,128)(2,1)} %get-tuple-element.156), kind=kOutput, calls=%fused_computation.195.clone.1 | convolution fusion | flops 77595648 | bytes 10626048 | tf_op jit(solution)/shard_map/while/body/eval_jaxpr/sub | solution.py:45
  337.2 4.7 %fusion.198 = bf16[16,2,1024,16]{2,3,1,0:T(8,128)(2,1)} fusion(bf16[16,2,1024,16]{2,3,1,0:T(8,128)(2,1)} %get-tuple-element.147, s32[]{:T(128)} %get-tuple-element.146, f32[2,1024,1024]{1,2,0:T(8,128)} %get-tuple-element.137, f32[2,1024]{1,0:T(2,128)S(1)} %get-tuple-element.138, bf16[16,2,1024,16]{2,3,1,0:T(8,128)(2,1)} %get-tuple-element.158), kind=kOutput, calls=%fused_computation.16.clone.1 | convolution fusion | flops 71335936 | bytes 8528896 | tf_op jit(solution)/shard_map/while/body/eval_jaxpr/hqk,hkd->hqd/dot_general | solution.py:47
  346.5 5.7 %fusion.52 = bf16[4096,128]{0,1:T(8,128)(2,1)S(1)} fusion(f32[4096,128]{0,1:T(8,128)} %copy-done.2, bf16[512,128]{1,0:T(8,128)(2,1)S(1)} %copy-done, bf16[128,512]{1,0:T(8,128)(2,1)S(1)} %copy-done.27, f32[128]{0:T(128)S(1)} %copy-done.28, f32[4096]{0:T(1024)S(1)} %add_rsqrt_fusion, f32[4096]{0:T(1024)S(1)} %broadcast_multiply_fusion), kind=kOutput, calls=%fused_computation.77 | convolution fusion | flops 1095761920 | bytes 3441152 | tf_op jit(solution)/shard_map/dot_general | solution.py:118
  353.0 15.1 %gather_fusion.2 = bf16[5120,128]{1,0:T(8,128)(2,1)S(1)} fusion(bf16[4096,128]{1,0:T(8,128)(2,1)S(1)} %copy.50, s32[5120]{0:T(1024)S(1)} %copy-done.17), kind=kCustom, calls=%fused_computation.2 | custom fusion | bytes 2641920 | tf_op jit(solution)/shard_map/jit(_take)/gather | solution.py:129
  370.1 33.1 %all_to_all.5 = bf16[128,40,128]{2,1,0:T(8,128)(2,1)S(1)} all-to-all(bf16[128,40,128]{2,1,0:T(8,128)(2,1)S(1)} %select_select_fusion), channel_id=1, replica_groups=mesh['gx'=8,'gy'=16] {'gx','gy'}, dimensions={0} | all-to-all | bytes 2621440 | tf_op jit(solution)/shard_map/all_to_all | solution.py:131
  (176 shorter events, 66.3 us)
Async XLA Ops:
  0.0 346.5 %copy-start = (bf16[512,128]{1,0:T(8,128)(2,1)S(1)}, bf16[512,128]{1,0:T(8,128)(2,1)}, u32[]{:S(2)}) copy-start(bf16[512,128]{1,0:T(8,128)(2,1)} %param.31) | copy-start | bytes 393220
  0.0 10.7 %copy-start.18 = (s32[1,4096]{1,0:T(1,128)S(1)}, s32[1,4096]{1,0:T(1,128)}, u32[]{:S(2)}) copy-start(s32[1,4096]{1,0:T(1,128)} %param.19) | copy-start | bytes 49156
  0.0 10.8 %copy-start.24 = (s32[1,128]{1,0:T(1,128)S(1)}, s32[1,128]{1,0:T(1,128)}, u32[]{:S(2)}) copy-start(s32[1,128]{1,0:T(1,128)} %param.22) | copy-start | bytes 1540
  0.0 11.4 %copy-start.1 = (s32[1,4096]{1,0:T(1,128)S(1)}, s32[1,4096]{1,0:T(1,128)}, u32[]{:S(2)}) copy-start(s32[1,4096]{1,0:T(1,128)} %param.21) | copy-start | bytes 49156
  4.2 40.1 %collective-permute-start = (bf16[1,16,16,128]{3,2,1,0:T(8,128)(2,1)S(1)}, bf16[1,16,16,128]{3,2,1,0:T(8,128)(2,1)S(1)}, u32[]{:S(2)}, u32[]{:S(2)}) collective-permute-start(bf16[1,16,16,128]{3,2,1,0:T(8,128)(2,1)S(1)} %bitcast.267), channel_id=1, source_target_pairs={{0,16},{16,32},{32,48},{48,64},{64,80},{80,96},{96,112},{1,17},{17... | collective-permute-start | bytes 196616 | tf_op jit(solution)/shard_map/ppermute | solution.py:21
  8.8 35.5 %collective-permute-start.1 = (bf16[1,16,16,128]{3,2,1,0:T(8,128)(2,1)S(1)}, bf16[1,16,16,128]{3,2,1,0:T(8,128)(2,1)S(1)}, u32[]{:S(2)}, u32[]{:S(2)}) collective-permute-start(bf16[1,16,16,128]{3,2,1,0:T(8,128)(2,1)S(1)} %bitcast.266), channel_id=1, source_target_pairs={{16,0},{32,16},{48,32},{64,48},{80,64},{96,80},{112,96},{17,1},{33... | collective-permute-start | bytes 196616 | tf_op jit(solution)/shard_map/ppermute | solution.py:22
  11.4 30.0 %copy-start.23 = (s32[1,4096]{1,0:T(1,128)S(1)}, s32[1,4096]{1,0:T(1,128)}, u32[]{:S(2)}) copy-start(s32[1,4096]{1,0:T(1,128)} %param.20) | copy-start | bytes 49156
  11.5 31.4 %copy-start.12 = (bf16[4096,128]{1,0:T(8,128)(2,1)S(1)}, bf16[4096,128]{1,0:T(8,128)(2,1)}, u32[]{:S(2)}) copy-start(bf16[4096,128]{1,0:T(8,128)(2,1)} %param.17) | copy-start | bytes 3145732
  44.3 6.0 %collective-permute-start.2 = (bf16[18,1,16,128]{3,2,1,0:T(8,128)(2,1)S(1)}, bf16[18,1,16,128]{3,2,1,0:T(8,128)(2,1)S(1)}, u32[]{:S(2)}, u32[]{:S(2)}) collective-permute-start(bf16[18,1,16,128]{3,2,1,0:T(8,128)(2,1)S(1)} %get-tuple-element.81), channel_id=1, source_target_pairs={{0,1},{1,2},{2,3},{3,4},{4,5},{5,6},{6,7},{7,8},{8,9},{9,10},{10,1... | collective-permute-start | bytes 221192 | tf_op jit(solution)/shard_map/ppermute | solution.py:21
  47.9 5.3 %collective-permute-start.3 = (bf16[18,1,16,128]{3,2,1,0:T(8,128)(2,1)S(1)}, bf16[18,1,16,128]{3,2,1,0:T(8,128)(2,1)S(1)}, u32[]{:S(2)}, u32[]{:S(2)}) collective-permute-start(bf16[18,1,16,128]{3,2,1,0:T(8,128)(2,1)S(1)} %get-tuple-element.82), channel_id=1, source_target_pairs={{1,0},{2,1},{3,2},{4,3},{5,4},{6,5},{7,6},{8,7},{9,8},{10,9},{11,1... | collective-permute-start | bytes 221192 | tf_op jit(solution)/shard_map/ppermute | solution.py:22
  61.5 1.7 copy-start.15
  65.3 1.2 copy-start.11
  66.5 1.2 copy-start.10
  67.8 1.2 copy-start.5
  69.0 1.2 copy-start.9
  70.6 1.2 copy-start.8
  71.9 1.2 copy-start.7
  73.5 1.2 copy-start.6
  74.7 1.2 copy-start.4
  76.4 1.2 copy-start.3
  82.3 1.8 copy-start.13
  82.3 1.8 copy-start.22
  86.6 1.2 copy-start.14
  86.6 1.2 copy-start.26
  107.8 0.9 copy-start.16
  107.8 0.9 copy-start.25
  341.9 2.4 copy-start.21
  344.9 1.3 copy-start.2
  344.9 1.6 copy-start.27
  344.9 1.6 copy-start.28
  352.3 0.7 copy-start.17
  353.0 15.1 %copy-start.19 = (pred[128,40]{1,0:T(8,128)(4,1)S(1)}, pred[128,40]{1,0:T(8,128)(4,1)}, u32[]{:S(2)}) copy-start(pred[128,40]{1,0:T(8,128)(4,1)} %get-tuple-element.96) | copy-start | bytes 15364
  353.0 15.1 %copy-start.20 = (pred[128,40]{1,0:T(8,128)(4,1)S(1)}, pred[128,40]{1,0:T(8,128)(4,1)}, u32[]{:S(2)}) copy-start(pred[128,40]{1,0:T(8,128)(4,1)} %get-tuple-element.97) | copy-start | bytes 15364
where the time goes:
time: 407 us; the launch traced here: 404 us
  matrix products  231 us (57%)
  local copies, waits for them, and re-layouts  105 us (26%)
  blocking collectives  33.1 us (8%)
  other arithmetic  20.5 us (5%)
  starting transfers between devices  11.4 us (3%)
    sub x16, matrix products, attend(): weights = jnp.where(allowed, jnp.exp(masked - row_peak), 0.0)  132 us
    dot_general x16, matrix products, attend(): jnp.einsum('hqk,hkd->hqd', attn_probs, values_in, preferred_element_type=...  75.5 us
    all_to_all x1, blocking collectives, body(): lax.all_to_all(send_buffer, ('gx', 'gy'), split_axis=0, concat_axis=0, ti...  33.1 us
    gather x2, local copies, waits for them, and re-layouts, body(): source_rows = jnp.take(hilbert_order[0], picks, axis=0)  28.7 us
    gather x2, local copies, waits for them, and re-layouts, body(): serial = jnp.take(residual, z_order[0], axis=0)  16.3 us
    gather x1, local copies, waits for them, and re-layouts, body(): jnp.take(block_out, source_rows, axis=0)  15.1 us
    dot_general x26, matrix products, body(): jnp.dot(piece, w_conv[tap], preferred_element_type=jnp.float32)  13.6 us
    unnamed x62, local copies, waits for them, and re-layouts  13.1 us
  transfers between devices with their start and end apart: 4, of which 1 were waited for; matrix products, arithmetic and copies ran while one was open for 9% of the time, Pallas kernels for 0%

commit v1 on v0

v1 whole, which is shorter than its diff:
```python
import functools
import jax
import jax.numpy as jnp
from jax import lax
from jax.experimental import pallas as pl
from jax.experimental.pallas import tpu as pltpu
from jax.sharding import PartitionSpec as P

C = 128
LA = 16
LB = 16
HEADS = 8
PATCH = 1024
HEAD_DIM = 16
QB = 256


def norm_rows(v, gain):
    center = v - jnp.mean(v, axis=-1, keepdims=True)
    spread = jnp.mean(center * center, axis=-1, keepdims=True)
    return center * lax.rsqrt(spread + 1e-05) * gain


def attn_kernel(zord, pad, res, gain, wqkv, wout, out, serial, qs, kt, va, heads, bd):
    rows = serial.shape[0]

    def gather(i, carry):
        base = i * 16
        for u in range(16):
            idx = zord[0, base + u]
            serial[pl.ds(base + u, 1), :] = res[pl.ds(idx, 1), :]
        return carry

    lax.fori_loop(0, rows // 16, gather, 0)

    va[:, C:] = jnp.ones((PATCH, C), jnp.bfloat16)
    sub = lax.broadcasted_iota(jnp.int32, (C, PATCH), 0)

    def patch(p, carry):
        off = pl.multiple_of(p * PATCH, PATCH)
        attn_in = norm_rows(serial[pl.ds(off, PATCH), :], gain[...]).astype(jnp.bfloat16)
        proj = jnp.dot(attn_in, wqkv[...], preferred_element_type=jnp.float32).astype(jnp.bfloat16)
        qs[...] = proj[:, :C] * jnp.bfloat16(HEAD_DIM ** -0.5)
        kt[:C, :] = proj[:, C : 2 * C].T
        va[:, :C] = proj[:, 2 * C :]
        bias = jnp.where(pad[:, pl.ds(off, PATCH)] > 0, 0.0, -1e30)
        kt[C:, :] = jnp.where(sub == 0, jnp.broadcast_to(bias, (C, PATCH)), 0.0).astype(jnp.bfloat16)
        rr = lax.broadcasted_iota(jnp.int32, (QB, QB), 0)
        cc = lax.broadcasted_iota(jnp.int32, (QB, QB), 1)
        for b in range(PATCH // QB):
            bd[b] = jnp.where(rr == cc, 0.0, bias[:, b * QB : (b + 1) * QB])

        def head(h, carry):
            lane = lax.broadcasted_iota(jnp.int32, (QB, C), 1)
            mine = lane // HEAD_DIM == h
            one = jnp.where(lane == 0, 1.0, 0.0).astype(jnp.bfloat16)
            for b in range(PATCH // QB):
                sl = slice(b * QB, (b + 1) * QB)
                q = jnp.where(mine, qs[sl, :], jnp.bfloat16(0))
                qa = jnp.concatenate([q, one], axis=1)
                parts = []
                for t in range(PATCH // QB):
                    ts = slice(t * QB, (t + 1) * QB)
                    if t == b:
                        parts.append(
                            jnp.dot(q, kt[:C, ts], preferred_element_type=jnp.float32) + bd[b]
                        )
                    else:
                        parts.append(jnp.dot(qa, kt[:, ts], preferred_element_type=jnp.float32))
                s = jnp.concatenate(parts, axis=1)
                peak = jnp.max(s, axis=-1, keepdims=True)
                prob = jnp.exp(s - peak).astype(jnp.bfloat16)
                o = jnp.dot(prob, va[...], preferred_element_type=jnp.float32)
                heads[sl, :] = jnp.where(mine, o[:, :C] / o[:, C:], heads[sl, :])
            return carry

        lax.fori_loop(0, HEADS, head, 0)
        rr = lax.broadcasted_iota(jnp.int32, (C, C), 0)
        cc = lax.broadcasted_iota(jnp.int32, (C, C), 1)
        part = jnp.dot(heads[...].astype(jnp.bfloat16), wout[...], preferred_element_type=jnp.float32)
        live = jnp.where(pad[:, pl.ds(off, PATCH)] > 0, 1.0, 0.0)
        for b in range(PATCH // C):
            diag = jnp.where(rr == cc, live[:, b * C : (b + 1) * C], 0.0).astype(jnp.bfloat16)
            col = jnp.dot(diag, jnp.ones((C, C), jnp.bfloat16), preferred_element_type=jnp.float32)
            at = pl.ds(off + b * C, C)
            out[at, :] = serial[at, :] + col * part[b * C : (b + 1) * C]
        return carry

    lax.fori_loop(0, rows // PATCH, patch, 0)


def attention(z_order, pad_mask, residual, gain, w_qkv, w_out):
    rows = residual.shape[0]
    vm = pl.BlockSpec(memory_space=pltpu.VMEM)
    return pl.pallas_call(
        attn_kernel,
        out_shape=jax.ShapeDtypeStruct((rows, C), jnp.float32),
        in_specs=[pl.BlockSpec(memory_space=pltpu.SMEM)] + [vm] * 5,
        out_specs=vm,
        scratch_shapes=[
            pltpu.VMEM((rows, C), jnp.float32),
            pltpu.VMEM((PATCH, C), jnp.bfloat16),
            pltpu.VMEM((2 * C, PATCH), jnp.bfloat16),
            pltpu.VMEM((PATCH, 2 * C), jnp.bfloat16),
            pltpu.VMEM((PATCH, C), jnp.float32),
            pltpu.VMEM((PATCH // QB, QB, QB), jnp.float32),
        ],
        compiler_params=pltpu.CompilerParams(vmem_limit_bytes=48 * 2**20),
        name="attention",
    )(z_order, pad_mask, residual, gain, w_qkv, w_out)


def moved_kernel(cap, per, hil, cnt, mixed, gain, wup, wdown, out, starts, rowbuf, send, send_sem, recv_sem, own_sem):
    n_x, n_y = lax.axis_size("gx"), lax.axis_size("gy")
    me_x, me_y = lax.axis_index("gx"), lax.axis_index("gy")
    me = me_x * n_y + me_y
    devices = n_x * n_y
    last = hil.shape[1] - 1

    def place(i):
        return lax.rem(me_x + i // n_y, n_x), lax.rem(me_y + i % n_y, n_y)

    barrier = pltpu.get_barrier_semaphore()

    def greet(i, carry):
        pl.semaphore_signal(barrier, inc=1, device_id=place(i), device_id_type=pl.DeviceIdType.MESH)
        return carry

    lax.fori_loop(1, devices, greet, 0)

    def offset(e, total):
        starts[e] = total
        return total + cnt[0, e]

    lax.fori_loop(0, devices, offset, jnp.int32(0))

    def compute(c):
        def rows_of(d, carry):
            to_x, to_y = place(c * per + d)
            start = starts[to_x * n_y + to_y]
            for j in range(cap):
                idx = hil[0, jnp.minimum(start + j, last)]
                rowbuf[pl.ds(d * cap + j, 1), :] = mixed[pl.ds(idx, 1), :]
            return carry

        lax.fori_loop(0, per, rows_of, 0)
        x = rowbuf[...]
        mlp_in = norm_rows(x, gain[...]).astype(jnp.bfloat16)
        up = jnp.dot(mlp_in, wup[...], preferred_element_type=jnp.float32)
        hidden = jax.nn.gelu(up).astype(jnp.bfloat16)
        y = x + jnp.dot(hidden, wdown[...], preferred_element_type=jnp.float32)
        slot = lax.broadcasted_iota(jnp.int32, (cap, C), 0)
        for d in range(per):
            to_x, to_y = place(c * per + d)
            count = cnt[0, to_x * n_y + to_y]
            send[c * per + d] = jnp.where(slot < count, y[d * cap : (d + 1) * cap], 0.0).astype(jnp.bfloat16)

    def copy(i):
        return pltpu.make_async_remote_copy(
            src_ref=send.at[i],
            dst_ref=out.at[me],
            send_sem=send_sem.at[i],
            recv_sem=recv_sem.at[i],
            device_id=place(i),
            device_id_type=pl.DeviceIdType.MESH,
        )

    def begin(i, carry):
        copy(i).start()
        return carry

    compute(0)
    own = pltpu.make_async_copy(send.at[0], out.at[me], own_sem)
    own.start()
    pl.semaphore_wait(barrier, devices - 1)
    lax.fori_loop(1, per, begin, 0)

    def step(c, carry):
        compute(c)
        lax.fori_loop(c * per, (c + 1) * per, begin, 0)
        return carry

    lax.fori_loop(1, devices // per, step, 0)
    own.wait()

    def finish(i, carry):
        copy(i).wait()
        return carry

    lax.fori_loop(1, devices, finish, 0)


def move_rows(hilbert_order, send_counts, mixed, gain, w_up, w_down, cap):
    devices = send_counts.shape[1]
    per = 8
    vm = pl.BlockSpec(memory_space=pltpu.VMEM)
    sm = pl.BlockSpec(memory_space=pltpu.SMEM)
    return pl.pallas_call(
        functools.partial(moved_kernel, cap, per),
        out_shape=jax.ShapeDtypeStruct((devices, cap, C), jnp.bfloat16),
        in_specs=[sm, sm] + [vm] * 4,
        out_specs=pl.BlockSpec(memory_space=pl.ANY),
        scratch_shapes=[
            pltpu.SMEM((devices,), jnp.int32),
            pltpu.VMEM((per * cap, C), jnp.float32),
            pltpu.VMEM((devices, cap, C), jnp.bfloat16),
            pltpu.SemaphoreType.DMA((devices,)),
            pltpu.SemaphoreType.DMA((devices,)),
            pltpu.SemaphoreType.DMA,
        ],
        compiler_params=pltpu.CompilerParams(
            vmem_limit_bytes=48 * 2**20, collective_id=1, has_side_effects=True
        ),
        name="move_rows",
    )(hilbert_order, send_counts, mixed, gain, w_up, w_down)


def padded(x, sides, width):
    for axis, dim in sides:
        devices, length = (lax.axis_size(axis), x.shape[dim])
        up = [(i, (i + 1) % devices) for i in range(devices - 1)]
        down = [(j, i) for i, j in up]
        last = lax.slice_in_dim(x, length - width, length, axis=dim)
        initial = lax.slice_in_dim(x, 0, width, axis=dim)
        before = lax.ppermute(last, axis, up)
        after = lax.ppermute(initial, axis, down)
        x = jnp.concatenate([before, x, after], axis=dim)
    return x


def body(
    points,
    occupied,
    z_order,
    pad_mask,
    hilbert_order,
    send_counts,
    w_conv,
    cpe_proj,
    cpe_gain,
    attn_gain,
    w_qkv,
    w_out,
    mlp_gain,
    w_up,
    w_down,
):
    point_count, width = points.shape
    depth = point_count // (LA * LB)
    filled = jnp.where(occupied[:, None] > 0, points, jnp.zeros_like(points))
    voxels = filled.reshape(LA, LB, depth, width)
    window = padded(voxels, (("gx", 0), ("gy", 1)), 1)
    window = jnp.pad(window, ((0, 0), (0, 0), (1, 1), (0, 0)))
    conv_sum = jnp.zeros((point_count, width), jnp.float32)
    for step_a in range(3):
        for step_b in range(3):
            for step_z in range(3):
                tap = step_a * 9 + step_b * 3 + step_z
                piece = window[
                    step_a : step_a + LA, step_b : step_b + LB, step_z : step_z + depth
                ].reshape(point_count, width)
                conv_sum = conv_sum + jnp.dot(
                    piece, w_conv[tap], preferred_element_type=jnp.float32
                )
    conv_out = conv_sum.astype(jnp.bfloat16)
    encoded = norm_rows(jnp.dot(conv_out, cpe_proj, preferred_element_type=jnp.float32), cpe_gain)
    residual = points.astype(jnp.float32) + encoded
    mixed = attention(
        z_order, pad_mask, residual, attn_gain.reshape(1, width), w_qkv, w_out
    )
    device_total = lax.axis_size("gx") * lax.axis_size("gy")
    capacity = point_count // device_total + max(2, point_count // (4 * device_total))
    received = move_rows(
        hilbert_order, send_counts, mixed, mlp_gain.reshape(1, width), w_up, w_down, capacity
    )
    return received.reshape(device_total * capacity, width)


def solution(mesh):
    placed = (
        P(("gx", "gy"), None),
        P(("gx", "gy")),
        P(("gx", "gy"), None),
        P(("gx", "gy"), None),
        P(("gx", "gy"), None),
        P(("gx", "gy"), None),
        P(),
        P(),
        P(),
        P(),
        P(),
        P(),
        P(),
        P(),
        P(),
    )
    return jax.shard_map(
        body, mesh=mesh, in_specs=placed, out_specs=P(("gx", "gy"), None), check_vma=False
    )
```

time: 407 us -> 169 us (0.42)
  matrix products: 231 us -> 15.2 us
  Pallas kernels: 0 us -> 102 us
  local copies, waits for them, and re-layouts: 105 us -> 21.3 us
  blocking collectives: 33.1 us -> 0 us
  other arithmetic: 20.5 us -> 11 us
    sub x16 -> x0, matrix products: 132 us -> none  [attend(): weights = jnp.where(allowed, jnp.exp(masked - row_peak), 0.0)]
    pallas_call x0 -> x2, Pallas kernels: none -> 102 us  [the longest x1 61.6 us: attention(): pl.pallas_call(attn_kernel, out_shape=jax.ShapeDtypeStruct((rows, C), jnp...]
    dot_general x19 -> x0, matrix products: 82.9 us -> none  [the longest x16 75.5 us: attend(): jnp.einsum('hqk,hkd->hqd', attn_probs, values_in, preferred_element_type=...]
    gather x5 -> x0, local copies, waits for them, and re-layouts: 60.2 us -> none  [the longest x2 28.7 us: body(): source_rows = jnp.take(hilbert_order[0], picks, axis=0)]
    all_to_all x1 -> x0, blocking collectives: 33.1 us -> none  [body(): lax.all_to_all(send_buffer, ('gx', 'gy'), split_axis=0, concat_axis=0, ti...]
    transpose x3 -> x0, local copies, waits for them, and re-layouts: 7.63 us -> none  [split_heads(): matrix.reshape(patch_count, PATCH, HEADS // 2, 2, HEAD_DIM)]
    reshape x5 -> x0, local copies, waits for them, and re-layouts: 6.82 us -> none  [the longest x3 4.75 us: split_heads(): matrix.reshape(patch_count, PATCH, HEADS // 2, 2, HEAD_DIM)]
    slice x4 -> x0, local copies, waits for them, and re-layouts: 6.34 us -> none  [the longest x2 3.38 us: body(): values_in = split_heads(projected[:, 2 * width:], patch_count)]
  transfers between devices with their start and end apart: 4 -> 4, of which waited for: 1 -> 2; matrix products, arithmetic and copies ran while one was open for 9% -> 1% of each run, Pallas kernels for 0% -> 0%
where the time goes in v1:
time: 169 us; the launch traced here: 168 us
  Pallas kernels  102 us (60%)
  local copies, waits for them, and re-layouts  21.3 us (13%)
  matrix products  15.2 us (9%)
  starting transfers between devices  11.4 us (7%)
  other arithmetic  11 us (7%)
  waiting for transfers between devices  6.51 us (4%)
    pallas_call x1, Pallas kernels, attention(): pl.pallas_call(attn_kernel, out_shape=jax.ShapeDtypeStruct((rows, C), jnp...  61.6 us
    pallas_call x1, Pallas kernels, move_rows(): pl.pallas_call(functools.partial(moved_kernel, cap, per), out_shape=jax.S...  40.3 us
    dot_general x26, matrix products, body(): jnp.dot(piece, w_conv[tap], preferred_element_type=jnp.float32)  12.2 us
    unnamed x55, local copies, waits for them, and re-layouts  10.8 us
    slice x2, local copies, waits for them, and re-layouts, body(): window[step_a:step_a + LA, step_b:step_b + LB, step_z:step_z + depth]  8.57 us
    ppermute x2, starting transfers between devices, padded(): before = lax.ppermute(last, axis, up)  8.14 us
    ppermute x2, waiting for transfers between devices, padded(): after = lax.ppermute(initial, axis, down)  6.51 us
  transfers between devices with their start and end apart: 4, of which 2 were waited for; matrix products, arithmetic and copies ran while one was open for 1% of the time, Pallas kernels for 0%

profile of v1, /device:TPU:1, one launch (start us, length us, event | category | flops | bytes accessed | tf_op | source)
XLA Modules:
  0.0 167.7 jit_solution(1200025385879067274)
XLA Ops:
  0.0 0.7 broadcast_compare_fusion
  0.7 3.4 %broadcast_select_fusion = bf16[4096,128]{1,0:T(8,128)(2,1)S(1)} fusion(bf16[4096,128]{1,0:T(8,128)(2,1)} %param.15, pred[4096]{0:T(1024)(128)(4,1)S(1)} %broadcast_compare_fusion), kind=kLoop, calls=%fused_computation.44 | loop fusion | flops 524288 | bytes 2101248 | tf_op jit(solution)/shard_map/jit(_where)/select_n | solution.py:250
  4.1 4.6 %collective-permute-start = (bf16[1,16,16,128]{3,2,1,0:T(8,128)(2,1)S(1)}, bf16[1,16,16,128]{3,2,1,0:T(8,128)(2,1)S(1)}, u32[]{:S(2)}, u32[]{:S(2)}) collective-permute-start(bf16[1,16,16,128]{3,2,1,0:T(8,128)(2,1)S(1)} %bitcast.178), channel_id=1, source_target_pairs={{0,16},{16,32},{32,48},{48,64},{64,80},{80,96},{96,112},{1,17},{17... | collective-permute-start | bytes 196616 | tf_op jit(solution)/shard_map/ppermute | solution.py:225
  8.7 1.9 %collective-permute-start.1 = (bf16[1,16,16,128]{3,2,1,0:T(8,128)(2,1)S(1)}, bf16[1,16,16,128]{3,2,1,0:T(8,128)(2,1)S(1)}, u32[]{:S(2)}, u32[]{:S(2)}) collective-permute-start(bf16[1,16,16,128]{3,2,1,0:T(8,128)(2,1)S(1)} %bitcast.177), channel_id=1, source_target_pairs={{16,0},{32,16},{48,32},{64,48},{80,64},{96,80},{112,96},{17,1},{33... | collective-permute-start | bytes 196616 | tf_op jit(solution)/shard_map/ppermute | solution.py:226
  10.7 3.6 %collective-permute-done.1 = bf16[1,16,16,128]{3,2,1,0:T(8,128)(2,1)S(1)} collective-permute-done((bf16[1,16,16,128]{3,2,1,0:T(8,128)(2,1)S(1)}, bf16[1,16,16,128]{3,2,1,0:T(8,128)(2,1)S(1)}, u32[]{:S(2)}, u32[]{:S(2)}) %collective-permute-start.1) | collective-permute-done | bytes 65568 | tf_op jit(solution)/shard_map/ppermute | solution.py:226
  14.3 3.5 %collective-permute-start.2 = (bf16[18,1,16,128]{3,2,1,0:T(8,128)(2,1)S(1)}, bf16[18,1,16,128]{3,2,1,0:T(8,128)(2,1)S(1)}, u32[]{:S(2)}, u32[]{:S(2)}) collective-permute-start(bf16[18,1,16,128]{3,2,1,0:T(8,128)(2,1)S(1)} %get-tuple-element.31), channel_id=1, source_target_pairs={{0,1},{1,2},{2,3},{3,4},{4,5},{5,6},{6,7},{7,8},{8,9},{9,10},{10,1... | collective-permute-start | bytes 221192 | tf_op jit(solution)/shard_map/ppermute | solution.py:225
  17.9 1.3 collective-permute-start.3
  19.2 1.1 pad_maximum_fusion.1
  20.3 2.9 %collective-permute-done.3 = bf16[18,1,16,128]{3,2,1,0:T(8,128)(2,1)S(1)} collective-permute-done((bf16[18,1,16,128]{3,2,1,0:T(8,128)(2,1)S(1)}, bf16[18,1,16,128]{3,2,1,0:T(8,128)(2,1)S(1)}, u32[]{:S(2)}, u32[]{:S(2)}) %collective-permute-start.3) | collective-permute-done | bytes 73760 | tf_op jit(solution)/shard_map/ppermute | solution.py:226
  23.2 1.8 %select_maximum_fusion = bf16[18,18,18,128]{3,2,1,0:T(8,128)(2,1)S(1)} fusion(bf16[18,1,16,128]{3,2,1,0:T(8,128)(2,1)S(1)} %collective-permute-done.3, bf16[18,1,16,128]{3,2,1,0:T(8,128)(2,1)S(1)} %collective-permute-done.2, bf16[1,16,16,128]{3,2,1,0:T(8,128)(2,1)S(1)} %collective-permute-done.1, bf16[16,16,16,128]{3,2,1,0:T(8,128)(2,1)S(1)} %bitcast.149, ...), kind=kLoop, calls=%fused_computation.32 | loop fusion | flops 13436928 | bytes 2820096 | tf_op jit(solution)/shard_map/concatenate | solution.py:227
  24.9 6.0 %fusion.69 = (bf16[16,16,16,128]{3,2,1,0:T(8,128)(2,1)}, bf16[16,16,16,128]{3,2,1,0:T(8,128)(2,1)S(1)}, bf16[16,16,16,128]{3,2,1,0:T(8,128)(2,1)S(1)}, bf16[16,1...) fusion(bf16[18,18,18,128]{3,2,1,0:T(8,128)(2,1)S(1)} %select_ma, ...), kind=kLoop, calls=%fused_computation.108 | loop fusion | bytes 37748736 | tf_op jit(solution)/shard_map/slice | solution.py:259
  31.0 1.8 %fusion.39 = f32[4096,128]{1,0:T(8,128)S(1)} fusion(bf16[4096,128]{1,0:T(8,128)(2,1)} %bitcast.174, bf16[27,128,128]{2,1,0:T(8,128)(2,1)} %param.21), kind=kOutput, calls=%fused_computation.76 | convolution fusion | flops 134217728 | bytes 3178496 | tf_op jit(solution)/shard_map/dot_general | solution.py:262
  33.4 2.6 %fusion.70 = (bf16[16,16,16,128]{3,2,1,0:T(8,128)(2,1)S(1)}, bf16[16,16,16,128]{3,2,1,0:T(8,128)(2,1)}, bf16[16,16,16,128]{3,2,1,0:T(8,128)(2,1)S(1)}, bf16[16,1...) fusion(bf16[18,17,16,128]{3,2,1,0:T(8,128)(2,1)S(1)} %get-tuple-element.29, ...), kind=kLoop, calls=%fused_computation.109 | loop fusion | bytes 12582912 | tf_op jit(solution)/shard_map/slice | solution.py:259
  36.0 0.4 convolution_add_fusion.23
  36.4 0.8 copy-done.20
  37.6 0.8 copy-done.19
  38.4 0.4 convolution_add_fusion.21
  38.9 0.8 copy-done.12
  40.1 0.8 copy-done.18
  41.7 0.8 copy-done.16
  42.5 0.4 convolution_add_fusion.17
  43.0 0.8 copy-done.15
  44.2 0.8 copy-done.21
  45.0 0.4 convolution_add_fusion.15
  45.4 0.8 copy-done.13
  46.6 0.8 copy-done.11
  47.8 0.4 convolution_add_fusion.12
  48.3 0.4 fusion.14
  48.7 0.4 convolution_add_fusion.11
  49.1 0.4 convolution_add_fusion.10
  49.5 0.8 copy-done.17
  50.3 0.4 convolution_add_fusion.9
  50.8 0.4 convolution_add_fusion.8
  51.2 0.4 convolution_add_fusion.7
  51.6 0.8 copy-done.14
  52.4 0.4 convolution_add_fusion.6
  52.8 0.4 convolution_add_fusion.5
  53.7 0.5 fusion
  54.1 0.4 convolution_add_fusion.2
  54.6 0.4 convolution_add_fusion.1
  55.0 0.8 copy-done.23
  55.8 3.0 %fusion.73 = (f32[4096]{0:T(1024)S(1)}, f32[4096,128]{0,1:T(8,128)}) fusion(bf16[128,128]{1,0:T(8,128)(2,1)S(1)} %copy-done, f32[4096,128]{1,0:T(8,128)S(1)} %convolution_add_fusion.1, bf16[4096,128]{1,0:T(8,128)(2,1)S(1)} %bitcast.176, bf16[27,128,128]{2,1,0:T(8,128)(2,1)} %param.21), kind=kOutput, calls=%fused_computation.112 | convolution fusion | flops 270004224 | bytes 5324800 | tf_op jit(solution)/shard_map/dot_general | solution.py:266
  58.8 1.9 %copy.16 = f32[4096,128]{1,0:T(8,128)S(1)} copy(f32[4096,128]{0,1:T(8,128)} %get-tuple-element.38) | data formatting | bytes 4194304 | tf_op jit(solution)/shard_map/dot_general | solution.py:266
  60.7 1.3 multiply_reduce_fusion
  62.1 2.5 %multiply_add_fusion.res = f32[4096,128]{1,0:T(8,128)S(1)} fusion(bf16[4096,128]{1,0:T(8,128)(2,1)S(1)} %copy-done.24, f32[4096,128]{1,0:T(8,128)S(1)} %copy.16, f32[128]{0:T(128)S(1)} %copy-done.26, f32[4096]{0:T(1024)S(1)} %add_rsqrt_fusion, f32[4096]{0:T(1024)S(1)} %broadcast_multiply_fusion), kind=kLoop, calls=%fused_computation.30 | loop fusion | flops 2621440 | bytes 5276160 | tf_op jit(solution)/shard_map/add | solution.py:267
  64.7 61.6 %attention.1.mixed = f32[4096,128]{1,0:T(8,128)S(1)} custom-call(s32[1,4096]{1,0:T(1,128)S(1)} %copy-done.5, s32[1,4096]{1,0:T(1,128)S(1)} %copy-done.6, f32[4096,128]{1,0:T(8,128)S(1)} %multiply_add_fusion.res, f32[1,128]{1,0:T(1,128)S(1)} %bitcast.145, bf16[128,384]{1,0:T(8,128)(2,1)S(1)} %copy-done.3, bf16[128,128]{1,0:T(8,128)(2,1)S(1)} %copy-done.4), custom_call_target="tpu_custom_call" | custom-call | tf_op jit(solution)/shard_map/attention/pallas_call | solution.py:95
  126.4 40.3 %move_rows.1 = bf16[128,40,128]{2,1,0:T(8,128)(2,1)S(1)} custom-call(s32[1,4096]{1,0:T(1,128)S(1)} %copy-done.7, s32[1,128]{1,0:T(1,128)S(1)} %copy-done.9, f32[4096,128]{1,0:T(8,128)S(1)} %attention.1.mixed, f32[1,128]{1,0:T(1,128)S(1)} %bitcast.146, bf16[128,512]{1,0:T(8,128)(2,1)S(1)} %copy-done.1, bf16[512,128]{1,0:T(8,128)(2,1)S(1)} %copy-done.2), custom_call_target="tpu_custom_call" | custom-call | tf_op jit(solution)/shard_map/move_rows/pallas_call | solution.py:198
  166.7 1.1 copy.18
  (58 shorter events, 4.1 us)
Async XLA Ops:
  0.0 55.0 %copy-start = (bf16[128,128]{1,0:T(8,128)(2,1)S(1)}, bf16[128,128]{1,0:T(8,128)(2,1)}, u32[]{:S(2)}) copy-start(bf16[128,128]{1,0:T(8,128)(2,1)} %param.22) | copy-start | bytes 98308
  4.1 6.5 %collective-permute-start = (bf16[1,16,16,128]{3,2,1,0:T(8,128)(2,1)S(1)}, bf16[1,16,16,128]{3,2,1,0:T(8,128)(2,1)S(1)}, u32[]{:S(2)}, u32[]{:S(2)}) collective-permute-start(bf16[1,16,16,128]{3,2,1,0:T(8,128)(2,1)S(1)} %bitcast.178), channel_id=1, source_target_pairs={{0,16},{16,32},{32,48},{48,64},{64,80},{80,96},{96,112},{1,17},{17... | collective-permute-start | bytes 196616 | tf_op jit(solution)/shard_map/ppermute | solution.py:225
  8.7 5.6 %collective-permute-start.1 = (bf16[1,16,16,128]{3,2,1,0:T(8,128)(2,1)S(1)}, bf16[1,16,16,128]{3,2,1,0:T(8,128)(2,1)S(1)}, u32[]{:S(2)}, u32[]{:S(2)}) collective-permute-start(bf16[1,16,16,128]{3,2,1,0:T(8,128)(2,1)S(1)} %bitcast.177), channel_id=1, source_target_pairs={{16,0},{32,16},{48,32},{64,48},{80,64},{96,80},{112,96},{17,1},{33... | collective-permute-start | bytes 196616 | tf_op jit(solution)/shard_map/ppermute | solution.py:226
  14.3 6.0 %collective-permute-start.2 = (bf16[18,1,16,128]{3,2,1,0:T(8,128)(2,1)S(1)}, bf16[18,1,16,128]{3,2,1,0:T(8,128)(2,1)S(1)}, u32[]{:S(2)}, u32[]{:S(2)}) collective-permute-start(bf16[18,1,16,128]{3,2,1,0:T(8,128)(2,1)S(1)} %get-tuple-element.31), channel_id=1, source_target_pairs={{0,1},{1,2},{2,3},{3,4},{4,5},{5,6},{6,7},{7,8},{8,9},{9,10},{10,1... | collective-permute-start | bytes 221192 | tf_op jit(solution)/shard_map/ppermute | solution.py:225
  17.9 5.3 %collective-permute-start.3 = (bf16[18,1,16,128]{3,2,1,0:T(8,128)(2,1)S(1)}, bf16[18,1,16,128]{3,2,1,0:T(8,128)(2,1)S(1)}, u32[]{:S(2)}, u32[]{:S(2)}) collective-permute-start(bf16[18,1,16,128]{3,2,1,0:T(8,128)(2,1)S(1)} %get-tuple-element.32), channel_id=1, source_target_pairs={{1,0},{2,1},{3,2},{4,3},{5,4},{6,5},{7,6},{8,7},{9,8},{10,9},{11,1... | collective-permute-start | bytes 221192 | tf_op jit(solution)/shard_map/ppermute | solution.py:226
  30.9 1.8 %copy-start.22 = (bf16[16,16,16,128]{3,2,1,0:T(8,128)(2,1)S(1)}, bf16[16,16,16,128]{3,2,1,0:T(8,128)(2,1)}, u32[]{:S(2)}) copy-start(bf16[16,16,16,128]{3,2,1,0:T(8,128)(2,1)} %get-tuple-element.19) | copy-start | bytes 3145732
  30.9 1.8 %copy-start.25 = (bf16[27,128,128]{2,1,0:T(8,128)(2,1)S(1)}, bf16[27,128,128]{2,1,0:T(8,128)(2,1)}, u32[]{:S(2)}) copy-start(bf16[27,128,128]{2,1,0:T(8,128)(2,1)} %param.21) | copy-start | bytes 2654212
  36.0 1.2 copy-start.20
  37.2 1.2 copy-start.19
  38.4 1.2 copy-start.12
  39.7 1.2 copy-start.18
  41.3 1.2 copy-start.16
  42.5 1.2 copy-start.15
  43.8 1.2 copy-start.21
  45.0 1.2 copy-start.13
  46.2 1.2 copy-start.11
  49.1 1.2 copy-start.17
  51.2 1.2 copy-start.14
  54.6 1.2 copy-start.23
  60.7 1.3 copy-start.24
  60.7 1.3 copy-start.26
  62.0 2.6 %copy-start.3 = (bf16[128,384]{1,0:T(8,128)(2,1)S(1)}, bf16[128,384]{1,0:T(8,128)(2,1)}, u32[]{:S(2)}) copy-start(bf16[128,384]{1,0:T(8,128)(2,1)} %wqkv.1) | copy-start | bytes 294916
  62.0 2.6 %copy-start.4 = (bf16[128,128]{1,0:T(8,128)(2,1)S(1)}, bf16[128,128]{1,0:T(8,128)(2,1)}, u32[]{:S(2)}) copy-start(bf16[128,128]{1,0:T(8,128)(2,1)} %wout.1) | copy-start | bytes 98308
  62.1 2.6 %copy-start.5 = (s32[1,4096]{1,0:T(1,128)S(1)}, s32[1,4096]{1,0:T(1,128)}, u32[]{:S(2)}) copy-start(s32[1,4096]{1,0:T(1,128)} %zord.1) | copy-start | bytes 49156
  62.1 2.6 %copy-start.6 = (s32[1,4096]{1,0:T(1,128)S(1)}, s32[1,4096]{1,0:T(1,128)}, u32[]{:S(2)}) copy-start(s32[1,4096]{1,0:T(1,128)} %pad.66) | copy-start | bytes 49156
  62.1 2.6 %copy-start.8 = (f32[128]{0:T(128)S(1)}, f32[128]{0:T(128)}, u32[]{:S(2)}) copy-start(f32[128]{0:T(128)} %param.24) | copy-start | bytes 1540
  64.7 61.7 %copy-start.1 = (bf16[128,512]{1,0:T(8,128)(2,1)S(1)}, bf16[128,512]{1,0:T(8,128)(2,1)}, u32[]{:S(2)}) copy-start(bf16[128,512]{1,0:T(8,128)(2,1)} %wup.1) | copy-start | bytes 393220
  64.7 61.7 %copy-start.2 = (bf16[512,128]{1,0:T(8,128)(2,1)S(1)}, bf16[512,128]{1,0:T(8,128)(2,1)}, u32[]{:S(2)}) copy-start(bf16[512,128]{1,0:T(8,128)(2,1)} %wdown.1) | copy-start | bytes 393220
  64.7 61.7 %copy-start.7 = (s32[1,4096]{1,0:T(1,128)S(1)}, s32[1,4096]{1,0:T(1,128)}, u32[]{:S(2)}) copy-start(s32[1,4096]{1,0:T(1,128)} %hil.1) | copy-start | bytes 49156
  64.7 61.7 %copy-start.9 = (s32[1,128]{1,0:T(1,128)S(1)}, s32[1,128]{1,0:T(1,128)}, u32[]{:S(2)}) copy-start(s32[1,128]{1,0:T(1,128)} %cnt.1) | copy-start | bytes 1540
  64.7 61.7 %copy-start.10 = (f32[128]{0:T(128)S(1)}, f32[128]{0:T(128)}, u32[]{:S(2)}) copy-start(f32[128]{0:T(128)} %param.27) | copy-start | bytes 1540

commit v2 on v1

--- a/solution.py
+++ b/solution.py
@@ -110,6 +110,166 @@
     )(z_order, pad_mask, residual, gain, w_qkv, w_out)
 
 
+def encode_kernel(pts, occ, wconv, proj, gain, out, win, taps, send_sem, recv_sem):
+    n_x, n_y = lax.axis_size("gx"), lax.axis_size("gy")
+    me_x, me_y = lax.axis_index("gx"), lax.axis_index("gy")
+    z = pts.shape[2]
+    cols = C // z
+    sides = [(dx, dy) for dx in (-1, 0, 1) for dy in (-1, 0, 1) if (dx, dy) != (0, 0)]
+
+    def place(dx, dy):
+        return lax.rem(me_x + (dx + n_x), n_x), lax.rem(me_y + (dy + n_y), n_y)
+
+    barrier = pltpu.get_barrier_semaphore()
+    for dx, dy in sides:
+        pl.semaphore_signal(barrier, inc=1, device_id=place(dx, dy), device_id_type=pl.DeviceIdType.MESH)
+
+    rr = lax.broadcasted_iota(jnp.int32, (C, C), 0)
+    cc = lax.broadcasted_iota(jnp.int32, (C, C), 1)
+
+    def pick(dz, row):
+        hit = (cc == rr + dz) & (rr // z == cc // z)
+        return jnp.where(hit, row, 0.0).astype(jnp.bfloat16)
+
+    def put(dz, a, b, block):
+        win[dz + 1, a, b] = block.astype(jnp.bfloat16).reshape(block.shape[0] // z, z, C)
+
+    def own_block(r):
+        a, b = r // 2, lax.rem(r, 2) * cols
+        row = jnp.where(occ[:, pl.ds(pl.multiple_of(r * C, C), C)] > 0, 1.0, 0.0)
+        return a, b, row, pts[a, pl.ds(b, cols)].reshape(C, C)
+
+    def fill(r, carry):
+        a, b, row, block = own_block(r)
+        put(0, a + 1, pl.ds(b + 1, cols), jnp.dot(pick(0, row), block, preferred_element_type=jnp.float32))
+        return carry
+
+    lax.fori_loop(0, LA * LB // cols, fill, 0)
+
+    def span(d, n):
+        here = {-1: pl.ds(1, 1), 0: pl.ds(1, n), 1: pl.ds(n, 1)}[d]
+        there = {-1: pl.ds(n + 1, 1), 0: pl.ds(1, n), 1: pl.ds(0, 1)}[d]
+        return here, there
+
+    copies = []
+    for k, (dx, dy) in enumerate(sides):
+        (from_a, to_a), (from_b, to_b) = span(dx, LA), span(dy, LB)
+        copies.append(
+            pltpu.make_async_remote_copy(
+                src_ref=win.at[1, from_a, from_b],
+                dst_ref=win.at[1, to_a, to_b],
+                send_sem=send_sem.at[k],
+                recv_sem=recv_sem.at[k],
+                device_id=place(dx, dy),
+                device_id_type=pl.DeviceIdType.MESH,
+            )
+        )
+    pl.semaphore_wait(barrier, len(sides))
+    for copy in copies:
+        copy.start()
+
+    def shift(r, carry):
+        a, b, row, block = own_block(r)
+        for dz in (-1, 1):
+            put(dz, a + 1, pl.ds(b + 1, cols), jnp.dot(pick(dz, row), block, preferred_element_type=jnp.float32))
+        return carry
+
+    lax.fori_loop(0, LA * LB // cols, shift, 0)
+
+    none = jnp.zeros((C, C), jnp.bfloat16)
+    for i in range(4):
+        for sb in range(3):
+            for sz in range(3):
+                at = ((i * 3 + sb) * 3 + sz) * C
+                taps[at : at + C, :C] = wconv[i * 9 + sb * 3 + sz] if i < 3 else none
+                taps[at : at + C, C:] = wconv[(i - 1) * 9 + sb * 3 + sz] if i > 0 else none
+
+    for copy in copies:
+        copy.wait()
+
+    low_x = jnp.where(me_x > 0, 1.0, 0.0)
+    high_x = jnp.where(me_x < n_x - 1, 1.0, 0.0)
+    low_y = jnp.where(me_y > 0, 1.0, 0.0)
+    high_y = jnp.where(me_y < n_y - 1, 1.0, 0.0)
+
+    def edge(a, b, count, live):
+        block = win[1, a, b].reshape(count * z, C)
+        for dz in (-1, 0, 1):
+            mat = pick(dz, live)[: count * z, : count * z]
+            put(dz, a, b, jnp.dot(mat, block, preferred_element_type=jnp.float32))
+
+    for half in range(2):
+        run = pl.ds(1 + half * cols, cols)
+        edge(0, run, cols, low_x)
+        edge(LA + 1, run, cols, high_x)
+        edge(run, 0, cols, low_y)
+        edge(run, LB + 1, cols, high_y)
+    for a, live_x in ((0, low_x), (LA + 1, high_x)):
+        for b, live_y in ((0, low_y), (LB + 1, high_y)):
+            edge(a, pl.ds(b, 1), 1, live_x * live_y)
+
+    tall = 2
+    wide = LB * z
+
+    def conv(t, carry):
+        total = None
+        for sb in range(3):
+            for pair in range(2):
+                pieces = []
+                for i in (2 * pair, 2 * pair + 1):
+                    for sz in range(3):
+                        pieces.append(
+                            jnp.concatenate(
+                                [
+                                    win[sz, (t * tall + u) * 2 + i, sb : sb + LB].reshape(wide, C)
+                                    for u in range(tall)
+                                ],
+                                axis=0,
+                            )
+                        )
+                w = jnp.concatenate(
+                    [taps[((i * 3 + sb) * 3) * C : ((i * 3 + sb) * 3 + 3) * C, :] for i in (2 * pair, 2 * pair + 1)],
+                    axis=0,
+                )
+                term = jnp.dot(jnp.concatenate(pieces, axis=1), w, preferred_element_type=jnp.float32)
+                total = term if total is None else total + term
+        for o in range(2):
+            conv_out = total[:, o * C : (o + 1) * C].astype(jnp.bfloat16)
+            encoded = norm_rows(
+                jnp.dot(conv_out, proj[...], preferred_element_type=jnp.float32), gain[...]
+            )
+            for u in range(tall):
+                a = (t * tall + u) * 2 + o
+                out[pl.ds(pl.multiple_of(a * wide, wide), wide), :] = (
+                    pts[a].reshape(wide, C).astype(jnp.float32) + encoded[u * wide : (u + 1) * wide]
+                )
+        return carry
+
+    lax.fori_loop(0, LA // 2 // tall, conv, 0)
+
+
+def encode(points, occupied, w_conv, cpe_proj, gain):
+    rows = points.shape[0]
+    depth = rows // (LA * LB)
+    vm = pl.BlockSpec(memory_space=pltpu.VMEM)
+    return pl.pallas_call(
+        encode_kernel,
+        out_shape=jax.ShapeDtypeStruct((rows, C), jnp.float32),
+        in_specs=[vm] * 5,
+        out_specs=vm,
+        scratch_shapes=[
+            pltpu.VMEM((3, LA + 2, LB + 2, depth, C), jnp.bfloat16),
+            pltpu.VMEM((36 * C, 2 * C), jnp.bfloat16),
+            pltpu.SemaphoreType.DMA((8,)),
+            pltpu.SemaphoreType.DMA((8,)),
+        ],
+        compiler_params=pltpu.CompilerParams(
+            vmem_limit_bytes=48 * 2**20, collective_id=0, has_side_effects=True
+        ),
+        name="encode",
+    )(points.reshape(LA, LB, depth, C), occupied.reshape(1, rows), w_conv, cpe_proj, gain)
+
+
 def moved_kernel(cap, per, hil, cnt, mixed, gain, wup, wdown, out, starts, rowbuf, send, send_sem, recv_sem, own_sem):
     n_x, n_y = lax.axis_size("gx"), lax.axis_size("gy")
     me_x, me_y = lax.axis_index("gx"), lax.axis_index("gy")
@@ -215,19 +375,6 @@
     )(hilbert_order, send_counts, mixed, gain, w_up, w_down)
 
 
-def padded(x, sides, width):
-    for axis, dim in sides:
-        devices, length = (lax.axis_size(axis), x.shape[dim])
-        up = [(i, (i + 1) % devices) for i in range(devices - 1)]
-        down = [(j, i) for i, j in up]
-        last = lax.slice_in_dim(x, length - width, length, axis=dim)
-        initial = lax.slice_in_dim(x, 0, width, axis=dim)
-        before = lax.ppermute(last, axis, up)
-        after = lax.ppermute(initial, axis, down)
-        x = jnp.concatenate([before, x, after], axis=dim)
-    return x
-
-
 def body(
     points,
     occupied,
@@ -246,25 +393,7 @@
     w_down,
 ):
     point_count, width = points.shape
-    depth = point_count // (LA * LB)
-    filled = jnp.where(occupied[:, None] > 0, points, jnp.zeros_like(points))
-    voxels = filled.reshape(LA, LB, depth, width)
-    window = padded(voxels, (("gx", 0), ("gy", 1)), 1)
-    window = jnp.pad(window, ((0, 0), (0, 0), (1, 1), (0, 0)))
-    conv_sum = jnp.zeros((point_count, width), jnp.float32)
-    for step_a in range(3):
-        for step_b in range(3):
-            for step_z in range(3):
-                tap = step_a * 9 + step_b * 3 + step_z
-                piece = window[
-                    step_a : step_a + LA, step_b : step_b + LB, step_z : step_z + depth
-                ].reshape(point_count, width)
-                conv_sum = conv_sum + jnp.dot(
-                    piece, w_conv[tap], preferred_element_type=jnp.float32
-                )
-    conv_out = conv_sum.astype(jnp.bfloat16)
-    encoded = norm_rows(jnp.dot(conv_out, cpe_proj, preferred_element_type=jnp.float32), cpe_gain)
-    residual = points.astype(jnp.float32) + encoded
+    residual = encode(points, occupied, w_conv, cpe_proj, cpe_gain.reshape(1, width))
     mixed = attention(
         z_order, pad_mask, residual, attn_gain.reshape(1, width), w_qkv, w_out
     )

time: 169 us -> 127 us (0.75)
  Pallas kernels: 102 us -> 121 us
  local copies, waits for them, and re-layouts: 21.3 us -> 5.64 us
  matrix products: 15.2 us -> 0 us
  starting transfers between devices: 11.4 us -> 0 us
  other arithmetic: 11 us -> 0 us
  waiting for transfers between devices: 6.51 us -> 0 us
    pallas_call x0 -> x1, Pallas kernels: none -> 22.4 us  [encode(): pl.pallas_call(encode_kernel, out_shape=jax.ShapeDtypeStruct((rows, C), j...]
    dot_general x27 -> x0, matrix products: 15.2 us -> none  [the longest x26 12.2 us: body(): jnp.dot(piece, w_conv[tap], preferred_element_type=jnp.float32)]
    ppermute x4 -> x0, starting transfers between devices: 11.4 us -> none  [the longest x2 8.14 us: padded(): before = lax.ppermute(last, axis, up)]
    slice x3 -> x0, local copies, waits for them, and re-layouts: 8.58 us -> none  [the longest x2 8.57 us: body(): window[step_a:step_a + LA, step_b:step_b + LB, step_z:step_z + depth]]
    ppermute x4 -> x0, waiting for transfers between devices: 6.51 us -> none  [the longest x2 6.51 us: padded(): after = lax.ppermute(initial, axis, down)]
    unnamed x55 -> x31, local copies, waits for them, and re-layouts: 10.8 us -> 5.64 us
    select_n x1 -> x0, other arithmetic: 3.37 us -> none  [body(): filled = jnp.where(occupied[:, None] > 0, points, jnp.zeros_like(points))]
    pallas_call x1, Pallas kernels: 40.3 us -> 37.1 us  [move_rows(): pl.pallas_call(functools.partial(moved_kernel, cap, per), out_shape=jax.S...]
  transfers between devices with their start and end apart: 4 -> 0, of which waited for: 2 -> 0; matrix products, arithmetic and copies ran while one was open for 1% -> 0% of each run, Pallas kernels for 0% -> 0%
where the time goes in v2:
time: 127 us
  Pallas kernels  121 us (95%)
  local copies, waits for them, and re-layouts  5.64 us (4%)
    pallas_call x1, Pallas kernels, attention(): pl.pallas_call(attn_kernel, out_shape=jax.ShapeDtypeStruct((rows, C), jnp...  61.6 us
    pallas_call x1, Pallas kernels, move_rows(): pl.pallas_call(functools.partial(moved_kernel, cap, per), out_shape=jax.S...  37.1 us
    pallas_call x1, Pallas kernels, encode(): pl.pallas_call(encode_kernel, out_shape=jax.ShapeDtypeStruct((rows, C), j...  22.4 us
    unnamed x31, local copies, waits for them, and re-layouts  5.64 us

profile of v2, /device:TPU:1, one launch (start us, length us, event | category | flops | bytes accessed | tf_op | source)
XLA Modules:
  0.0 126.9 jit_solution(7105991161459487104)
XLA Ops:
  0.0 0.0 copy-start.12
  0.0 0.0 copy-start
  0.0 1.2 copy-done
  1.2 0.0 copy-start.1
  1.2 1.2 copy-done.1
  2.4 0.0 copy-start.5
  2.4 0.8 copy-done.5
  3.2 0.0 copy-start.7
  3.2 0.7 copy-done.7
  3.9 0.0 copy-start.11
  3.9 0.7 copy-done.11
  4.5 0.0 copy-start.4
  4.5 0.0 copy-start.6
  4.5 0.0 copy-start.8
  4.5 0.0 copy-start.9
  4.6 22.4 %encode.1.res = f32[4096,128]{1,0:T(8,128)S(1)} custom-call(bf16[16,16,16,128]{3,2,1,0:T(8,128)(2,1)S(1)} %bitcast.7, s32[1,4096]{1,0:T(1,128)S(1)} %bitcast.8, bf16[27,128,128]{2,1,0:T(8,128)(2,1)S(1)} %copy-done.1, bf16[128,128]{1,0:T(8,128)(2,1)S(1)} %copy-done.5, f32[1,128]{1,0:T(1,128)S(1)} %bitcast.9), custom_call_target="tpu_custom_call" | custom-call | tf_op jit(solution)/shard_map/encode/pallas_call | solution.py:255
  26.9 0.0 copy-done.12
  27.0 0.0 copy-done.4
  27.0 0.0 copy-done.6
  27.0 0.0 copy-done.8
  27.0 0.0 copy-done.9
  27.0 0.0 copy-start.2
  27.0 0.0 copy-start.3
  27.0 0.0 copy-start.10
  27.0 0.0 copy-start.13
  27.0 0.0 copy-start.14
  27.1 61.6 %attention.1.mixed = f32[4096,128]{1,0:T(8,128)S(1)} custom-call(s32[1,4096]{1,0:T(1,128)S(1)} %copy-done.8, s32[1,4096]{1,0:T(1,128)S(1)} %copy-done.9, f32[4096,128]{1,0:T(8,128)S(1)} %encode.1.res, f32[1,128]{1,0:T(1,128)S(1)} %bitcast.10, bf16[128,384]{1,0:T(8,128)(2,1)S(1)} %copy-done.4, bf16[128,128]{1,0:T(8,128)(2,1)S(1)} %copy-done.6), custom_call_target="tpu_custom_call" | custom-call | tf_op jit(solution)/shard_map/attention/pallas_call | solution.py:95
  88.7 0.0 copy-done.2
  88.7 0.0 copy-done.3
  88.7 0.0 copy-done.10
  88.7 0.0 copy-done.13
  88.7 0.0 copy-done.14
  88.7 37.1 %move_rows.1 = bf16[128,40,128]{2,1,0:T(8,128)(2,1)S(1)} custom-call(s32[1,4096]{1,0:T(1,128)S(1)} %copy-done.10, s32[1,128]{1,0:T(1,128)S(1)} %copy-done.13, f32[4096,128]{1,0:T(8,128)S(1)} %attention.1.mixed, f32[1,128]{1,0:T(1,128)S(1)} %bitcast.11, bf16[128,512]{1,0:T(8,128)(2,1)S(1)} %copy-done.2, bf16[512,128]{1,0:T(8,128)(2,1)S(1)} %copy-done.3), custom_call_target="tpu_custom_call" | custom-call | tf_op jit(solution)/shard_map/move_rows/pallas_call | solution.py:358
  125.8 1.1 copy.17
Async XLA Ops:
  0.0 26.9 %copy-start.12 = (f32[128]{0:T(128)S(1)}, f32[128]{0:T(128)}, u32[]{:S(2)}) copy-start(f32[128]{0:T(128)} %param.24) | copy-start | bytes 1540
  0.0 1.2 copy-start
  1.2 1.2 copy-start.1
  2.4 0.8 copy-start.5
  3.2 0.7 copy-start.7
  3.9 0.7 copy-start.11
  4.5 22.4 %copy-start.4 = (bf16[128,384]{1,0:T(8,128)(2,1)S(1)}, bf16[128,384]{1,0:T(8,128)(2,1)}, u32[]{:S(2)}) copy-start(bf16[128,384]{1,0:T(8,128)(2,1)} %wqkv.1) | copy-start | bytes 294916
  4.5 22.4 %copy-start.6 = (bf16[128,128]{1,0:T(8,128)(2,1)S(1)}, bf16[128,128]{1,0:T(8,128)(2,1)}, u32[]{:S(2)}) copy-start(bf16[128,128]{1,0:T(8,128)(2,1)} %wout.1) | copy-start | bytes 98308
  4.5 22.4 %copy-start.8 = (s32[1,4096]{1,0:T(1,128)S(1)}, s32[1,4096]{1,0:T(1,128)}, u32[]{:S(2)}) copy-start(s32[1,4096]{1,0:T(1,128)} %zord.1) | copy-start | bytes 49156
  4.5 22.4 %copy-start.9 = (s32[1,4096]{1,0:T(1,128)S(1)}, s32[1,4096]{1,0:T(1,128)}, u32[]{:S(2)}) copy-start(s32[1,4096]{1,0:T(1,128)} %pad.1) | copy-start | bytes 49156
  27.0 61.7 %copy-start.2 = (bf16[128,512]{1,0:T(8,128)(2,1)S(1)}, bf16[128,512]{1,0:T(8,128)(2,1)}, u32[]{:S(2)}) copy-start(bf16[128,512]{1,0:T(8,128)(2,1)} %wup.1) | copy-start | bytes 393220
  27.0 61.7 %copy-start.3 = (bf16[512,128]{1,0:T(8,128)(2,1)S(1)}, bf16[512,128]{1,0:T(8,128)(2,1)}, u32[]{:S(2)}) copy-start(bf16[512,128]{1,0:T(8,128)(2,1)} %wdown.1) | copy-start | bytes 393220
  27.0 61.7 %copy-start.10 = (s32[1,4096]{1,0:T(1,128)S(1)}, s32[1,4096]{1,0:T(1,128)}, u32[]{:S(2)}) copy-start(s32[1,4096]{1,0:T(1,128)} %hil.1) | copy-start | bytes 49156
  27.0 61.7 %copy-start.13 = (s32[1,128]{1,0:T(1,128)S(1)}, s32[1,128]{1,0:T(1,128)}, u32[]{:S(2)}) copy-start(s32[1,128]{1,0:T(1,128)} %cnt.1) | copy-start | bytes 1540
  27.0 61.7 %copy-start.14 = (f32[128]{0:T(128)S(1)}, f32[128]{0:T(128)}, u32[]{:S(2)}) copy-start(f32[128]{0:T(128)} %param.27) | copy-start | bytes 1540

commit v3 on v2

--- a/solution.py
+++ b/solution.py
@@ -1,4 +1,5 @@
 import functools
+import math
 import jax
 import jax.numpy as jnp
 from jax import lax
@@ -13,6 +14,7 @@
 PATCH = 1024
 HEAD_DIM = 16
 QB = 256
+UNROLL = 2
 
 
 def norm_rows(v, gain):
@@ -21,8 +23,10 @@
     return center * lax.rsqrt(spread + 1e-05) * gain
 
 
-def attn_kernel(zord, pad, res, gain, wqkv, wout, out, serial, qs, kt, va, heads, bd):
+def attn_kernel(zord, pad, res, gain, wqkv, wout, out, serial, qw, ka, vt, heads, live, bd, sbuf):
     rows = serial.shape[0]
+    blocks = PATCH // QB
+    half = C // 2
 
     def gather(i, carry):
         base = i * 16
@@ -33,57 +37,98 @@
 
     lax.fori_loop(0, rows // 16, gather, 0)
 
-    va[:, C:] = jnp.ones((PATCH, C), jnp.bfloat16)
-    sub = lax.broadcasted_iota(jnp.int32, (C, PATCH), 0)
+    first = lax.broadcasted_iota(jnp.int32, (HEAD_DIM, PATCH), 0) == 0
+    unit = jnp.where(first, 1.0, 0.0).astype(jnp.bfloat16)
+    for h in range(HEADS):
+        qw[h] = jnp.zeros((2 * C, PATCH), jnp.bfloat16)
+        qw[h, 3 * half : 3 * half + HEAD_DIM] = unit
+        vt[h, HEAD_DIM:] = unit
 
     def patch(p, carry):
         off = pl.multiple_of(p * PATCH, PATCH)
         attn_in = norm_rows(serial[pl.ds(off, PATCH), :], gain[...]).astype(jnp.bfloat16)
-        proj = jnp.dot(attn_in, wqkv[...], preferred_element_type=jnp.float32).astype(jnp.bfloat16)
-        qs[...] = proj[:, :C] * jnp.bfloat16(HEAD_DIM ** -0.5)
-        kt[:C, :] = proj[:, C : 2 * C].T
-        va[:, :C] = proj[:, 2 * C :]
-        bias = jnp.where(pad[:, pl.ds(off, PATCH)] > 0, 0.0, -1e30)
-        kt[C:, :] = jnp.where(sub == 0, jnp.broadcast_to(bias, (C, PATCH)), 0.0).astype(jnp.bfloat16)
+        proj = jnp.dot(attn_in, wqkv[...], preferred_element_type=jnp.float32)
+        proj = proj.astype(jnp.bfloat16).astype(jnp.float32)
+        qt = proj[:, :C].T * jnp.float32(HEAD_DIM ** -0.5 * math.log2(math.e))
+        high = qt.astype(jnp.bfloat16)
+        rest = qt - high.astype(jnp.float32)
+        mid = rest.astype(jnp.bfloat16)
+        low = (rest - mid.astype(jnp.float32)).astype(jnp.bfloat16)
+        vals = proj[:, 2 * C :].T.astype(jnp.bfloat16)
+        for h in range(HEADS):
+            sl = slice(h * HEAD_DIM, (h + 1) * HEAD_DIM)
+            at = h % 4 * HEAD_DIM
+            qw[h, at : at + HEAD_DIM] = high[sl]
+            qw[h, half + at : half + at + HEAD_DIM] = mid[sl]
+            qw[h, C + at : C + at + HEAD_DIM] = low[sl]
+            vt[h, :HEAD_DIM] = vals[sl]
+        rr = lax.broadcasted_iota(jnp.int32, (C, C), 0)
+        cc = lax.broadcasted_iota(jnp.int32, (C, C), 1)
+        real = jnp.where(pad[:, pl.ds(off, PATCH)] > 0, 1.0, 0.0)
+        for b in range(PATCH // C):
+            diag = jnp.where(rr == cc, real[:, b * C : (b + 1) * C], 0.0).astype(jnp.bfloat16)
+            live[b * C : (b + 1) * C] = jnp.dot(
+                diag, jnp.ones((C, C), jnp.bfloat16), preferred_element_type=jnp.float32
+            )
+        bias = (1.0 - live[...]) * -1e30
+        k = proj[:, C : 2 * C]
+        kr = pltpu.roll(k, half, 1)
+        left = lax.broadcasted_iota(jnp.int32, (PATCH, C), 1) < half
+        ka[0, :, :C] = jnp.where(left, k, kr).astype(jnp.bfloat16)
+        ka[0, :, C:] = jnp.where(left, k, bias).astype(jnp.bfloat16)
+        ka[1, :, :C] = jnp.where(left, kr, k).astype(jnp.bfloat16)
+        ka[1, :, C:] = jnp.where(left, kr, bias).astype(jnp.bfloat16)
         rr = lax.broadcasted_iota(jnp.int32, (QB, QB), 0)
         cc = lax.broadcasted_iota(jnp.int32, (QB, QB), 1)
-        for b in range(PATCH // QB):
-            bd[b] = jnp.where(rr == cc, 0.0, bias[:, b * QB : (b + 1) * QB])
-
-        def head(h, carry):
-            lane = lax.broadcasted_iota(jnp.int32, (QB, C), 1)
-            mine = lane // HEAD_DIM == h
-            one = jnp.where(lane == 0, 1.0, 0.0).astype(jnp.bfloat16)
-            for b in range(PATCH // QB):
-                sl = slice(b * QB, (b + 1) * QB)
-                q = jnp.where(mine, qs[sl, :], jnp.bfloat16(0))
-                qa = jnp.concatenate([q, one], axis=1)
+        for b in range(blocks):
+            col = bias[b * QB : (b + 1) * QB]
+            bd[b] = jnp.where(rr == cc, 0.0, jnp.concatenate([col, col], axis=1))
+
+        def scores(h, b, t):
+            g = h // 4
+            qs = slice(b * QB, (b + 1) * QB)
+            ts = slice(t * QB, (t + 1) * QB)
+            if t == b:
+                w = jnp.concatenate(
+                    [qw[h, : 3 * half, qs], jnp.zeros((half, QB), jnp.bfloat16)], axis=0
+                )
+                s = jnp.dot(ka[g, ts], w, preferred_element_type=jnp.float32) + bd[b]
+            else:
+                s = jnp.dot(ka[g, ts], qw[h, :, qs], preferred_element_type=jnp.float32)
+            sbuf[b % 2, ts] = s
+            return jnp.max(s.reshape(QB // 8, 8, QB), axis=0)
+
+        def values(h, b, t, peak):
+            ts = slice(t * QB, (t + 1) * QB)
+            prob = jnp.exp2(sbuf[b % 2, ts] - peak).astype(jnp.bfloat16)
+            return jnp.dot(vt[h, :, ts], prob, preferred_element_type=jnp.float32)
+
+        def top(parts):
+            m = functools.reduce(jnp.maximum, parts)
+            return jnp.max(m, axis=0, keepdims=True)
+
+        start = top([scores(0, 0, t) for t in range(blocks)])
+
+        def head(h, peak):
+            for b in range(blocks):
+                h2, b2 = (h, b + 1) if b + 1 < blocks else (lax.rem(h + 1, HEADS), 0)
                 parts = []
-                for t in range(PATCH // QB):
-                    ts = slice(t * QB, (t + 1) * QB)
-                    if t == b:
-                        parts.append(
-                            jnp.dot(q, kt[:C, ts], preferred_element_type=jnp.float32) + bd[b]
-                        )
-                    else:
-                        parts.append(jnp.dot(qa, kt[:, ts], preferred_element_type=jnp.float32))
-                s = jnp.concatenate(parts, axis=1)
-                peak = jnp.max(s, axis=-1, keepdims=True)
-                prob = jnp.exp(s - peak).astype(jnp.bfloat16)
-                o = jnp.dot(prob, va[...], preferred_element_type=jnp.float32)
-                heads[sl, :] = jnp.where(mine, o[:, :C] / o[:, C:], heads[sl, :])
-            return carry
-
-        lax.fori_loop(0, HEADS, head, 0)
-        rr = lax.broadcasted_iota(jnp.int32, (C, C), 0)
-        cc = lax.broadcasted_iota(jnp.int32, (C, C), 1)
-        part = jnp.dot(heads[...].astype(jnp.bfloat16), wout[...], preferred_element_type=jnp.float32)
-        live = jnp.where(pad[:, pl.ds(off, PATCH)] > 0, 1.0, 0.0)
-        for b in range(PATCH // C):
-            diag = jnp.where(rr == cc, live[:, b * C : (b + 1) * C], 0.0).astype(jnp.bfloat16)
-            col = jnp.dot(diag, jnp.ones((C, C), jnp.bfloat16), preferred_element_type=jnp.float32)
-            at = pl.ds(off + b * C, C)
-            out[at, :] = serial[at, :] + col * part[b * C : (b + 1) * C]
+                total = None
+                for t in range(blocks):
+                    parts.append(scores(h2, b2, t))
+                    term = values(h, b, t, peak)
+                    total = term if total is None else total + term
+                heads[pl.ds(pl.multiple_of(h * HEAD_DIM, HEAD_DIM), HEAD_DIM), b * QB : (b + 1) * QB] = (
+                    total[:HEAD_DIM] / total[HEAD_DIM : HEAD_DIM + 1]
+                )
+                peak = top(parts)
+            return peak
+
+        lax.fori_loop(0, HEADS, head, start, unroll=UNROLL)
+        mixed_heads = heads[...].T.astype(jnp.bfloat16)
+        part = jnp.dot(mixed_heads, wout[...], preferred_element_type=jnp.float32)
+        at = pl.ds(off, PATCH)
+        out[at, :] = serial[at, :] + live[...] * part
         return carry
 
     lax.fori_loop(0, rows // PATCH, patch, 0)
@@ -99,11 +144,13 @@
         out_specs=vm,
         scratch_shapes=[
             pltpu.VMEM((rows, C), jnp.float32),
-            pltpu.VMEM((PATCH, C), jnp.bfloat16),
-            pltpu.VMEM((2 * C, PATCH), jnp.bfloat16),
-            pltpu.VMEM((PATCH, 2 * C), jnp.bfloat16),
+            pltpu.VMEM((HEADS, 2 * C, PATCH), jnp.bfloat16),
+            pltpu.VMEM((2, PATCH, 2 * C), jnp.bfloat16),
+            pltpu.VMEM((HEADS, 2 * HEAD_DIM, PATCH), jnp.bfloat16),
+            pltpu.VMEM((C, PATCH), jnp.float32),
             pltpu.VMEM((PATCH, C), jnp.float32),
             pltpu.VMEM((PATCH // QB, QB, QB), jnp.float32),
+            pltpu.VMEM((2, PATCH, QB), jnp.float32),
         ],
         compiler_params=pltpu.CompilerParams(vmem_limit_bytes=48 * 2**20),
         name="attention",

time: 127 us -> 108 us (0.85)
  Pallas kernels: 121 us -> 102 us
    pallas_call x1, Pallas kernels: 61.6 us -> 42.5 us  [attention(): pl.pallas_call(attn_kernel, out_shape=jax.ShapeDtypeStruct((rows, C), jnp...]
where the time goes in v3:
time: 108 us
  Pallas kernels  102 us (94%)
  local copies, waits for them, and re-layouts  5.64 us (5%)
    pallas_call x1, Pallas kernels, attention(): pl.pallas_call(attn_kernel, out_shape=jax.ShapeDtypeStruct((rows, C), jnp...  42.5 us
    pallas_call x1, Pallas kernels, move_rows(): pl.pallas_call(functools.partial(moved_kernel, cap, per), out_shape=jax.S...  37.1 us
    pallas_call x1, Pallas kernels, encode(): pl.pallas_call(encode_kernel, out_shape=jax.ShapeDtypeStruct((rows, C), j...  22.4 us
    unnamed x31, local copies, waits for them, and re-layouts  5.64 us

profile of v3, /device:TPU:1, one launch (start us, length us, event | category | flops | bytes accessed | tf_op | source)
XLA Modules:
  0.0 107.8 jit_solution(16079221984861987027)
XLA Ops:
  0.0 0.0 copy-start.12
  0.0 0.0 copy-start
  0.0 1.2 %copy-done = bf16[4096,128]{1,0:T(8,128)(2,1)S(1)} copy-done((bf16[4096,128]{1,0:T(8,128)(2,1)S(1)}, bf16[4096,128]{1,0:T(8,128)(2,1)}, u32[]{:S(2)}) %copy-start) | copy-done | bytes 1048600
  1.2 0.0 copy-start.1
  1.2 1.2 %copy-done.1 = bf16[27,128,128]{2,1,0:T(8,128)(2,1)S(1)} copy-done((bf16[27,128,128]{2,1,0:T(8,128)(2,1)S(1)}, bf16[27,128,128]{2,1,0:T(8,128)(2,1)}, u32[]{:S(2)}) %copy-start.1) | copy-done | bytes 884760
  2.4 0.0 copy-start.5
  2.4 0.8 copy-done.5
  3.2 0.0 copy-start.7
  3.2 0.7 copy-done.7
  3.9 0.0 copy-start.11
  3.9 0.7 copy-done.11
  4.5 0.0 copy-start.4
  4.5 0.0 copy-start.6
  4.5 0.0 copy-start.8
  4.5 0.0 copy-start.9
  4.6 22.4 %encode.1.res = f32[4096,128]{1,0:T(8,128)S(1)} custom-call(bf16[16,16,16,128]{3,2,1,0:T(8,128)(2,1)S(1)} %bitcast.7, s32[1,4096]{1,0:T(1,128)S(1)} %bitcast.8, bf16[27,128,128]{2,1,0:T(8,128)(2,1)S(1)} %copy-done.1, bf16[128,128]{1,0:T(8,128)(2,1)S(1)} %copy-done.5, f32[1,128]{1,0:T(1,128)S(1)} %bitcast.9), custom_call_target="tpu_custom_call" | custom-call | tf_op jit(solution)/shard_map/encode/pallas_call | solution.py:302
  26.9 0.0 copy-done.12
  27.0 0.0 copy-done.4
  27.0 0.0 copy-done.6
  27.0 0.0 copy-done.8
  27.0 0.0 copy-done.9
  27.0 0.0 copy-start.2
  27.0 0.0 copy-start.3
  27.0 0.0 copy-start.10
  27.0 0.0 copy-start.13
  27.0 0.0 copy-start.14
  27.1 42.5 %attention.1.mixed = f32[4096,128]{1,0:T(8,128)S(1)} custom-call(s32[1,4096]{1,0:T(1,128)S(1)} %copy-done.8, s32[1,4096]{1,0:T(1,128)S(1)} %copy-done.9, f32[4096,128]{1,0:T(8,128)S(1)} %encode.1.res, f32[1,128]{1,0:T(1,128)S(1)} %bitcast.10, bf16[128,384]{1,0:T(8,128)(2,1)S(1)} %copy-done.4, bf16[128,128]{1,0:T(8,128)(2,1)S(1)} %copy-done.6), custom_call_target="tpu_custom_call" | custom-call | tf_op jit(solution)/shard_map/attention/pallas_call | solution.py:140
  69.6 0.0 copy-done.2
  69.6 0.0 copy-done.3
  69.6 0.0 copy-done.10
  69.6 0.0 copy-done.13
  69.7 0.0 copy-done.14
  69.7 37.1 %move_rows.1 = bf16[128,40,128]{2,1,0:T(8,128)(2,1)S(1)} custom-call(s32[1,4096]{1,0:T(1,128)S(1)} %copy-done.10, s32[1,128]{1,0:T(1,128)S(1)} %copy-done.13, f32[4096,128]{1,0:T(8,128)S(1)} %attention.1.mixed, f32[1,128]{1,0:T(1,128)S(1)} %bitcast.11, bf16[128,512]{1,0:T(8,128)(2,1)S(1)} %copy-done.2, bf16[512,128]{1,0:T(8,128)(2,1)S(1)} %copy-done.3), custom_call_target="tpu_custom_call" | custom-call | tf_op jit(solution)/shard_map/move_rows/pallas_call | solution.py:405
  106.8 1.1 copy.17
Async XLA Ops:
  0.0 26.9 %copy-start.12 = (f32[128]{0:T(128)S(1)}, f32[128]{0:T(128)}, u32[]{:S(2)}) copy-start(f32[128]{0:T(128)} %param.24) | copy-start | bytes 1540
  0.0 1.2 %copy-start = (bf16[4096,128]{1,0:T(8,128)(2,1)S(1)}, bf16[4096,128]{1,0:T(8,128)(2,1)}, u32[]{:S(2)}) copy-start(bf16[4096,128]{1,0:T(8,128)(2,1)} %param.15) | copy-start | bytes 3145732
  1.2 1.2 %copy-start.1 = (bf16[27,128,128]{2,1,0:T(8,128)(2,1)S(1)}, bf16[27,128,128]{2,1,0:T(8,128)(2,1)}, u32[]{:S(2)}) copy-start(bf16[27,128,128]{2,1,0:T(8,128)(2,1)} %wconv.1) | copy-start | bytes 2654212
  2.4 0.8 copy-start.5
  3.2 0.7 copy-start.7
  3.9 0.7 copy-start.11
  4.5 22.4 %copy-start.4 = (bf16[128,384]{1,0:T(8,128)(2,1)S(1)}, bf16[128,384]{1,0:T(8,128)(2,1)}, u32[]{:S(2)}) copy-start(bf16[128,384]{1,0:T(8,128)(2,1)} %wqkv.1) | copy-start | bytes 294916
  4.5 22.4 %copy-start.6 = (bf16[128,128]{1,0:T(8,128)(2,1)S(1)}, bf16[128,128]{1,0:T(8,128)(2,1)}, u32[]{:S(2)}) copy-start(bf16[128,128]{1,0:T(8,128)(2,1)} %wout.1) | copy-start | bytes 98308
  4.5 22.4 %copy-start.8 = (s32[1,4096]{1,0:T(1,128)S(1)}, s32[1,4096]{1,0:T(1,128)}, u32[]{:S(2)}) copy-start(s32[1,4096]{1,0:T(1,128)} %zord.1) | copy-start | bytes 49156
  4.5 22.4 %copy-start.9 = (s32[1,4096]{1,0:T(1,128)S(1)}, s32[1,4096]{1,0:T(1,128)}, u32[]{:S(2)}) copy-start(s32[1,4096]{1,0:T(1,128)} %pad.1) | copy-start | bytes 49156
  27.0 42.6 %copy-start.2 = (bf16[128,512]{1,0:T(8,128)(2,1)S(1)}, bf16[128,512]{1,0:T(8,128)(2,1)}, u32[]{:S(2)}) copy-start(bf16[128,512]{1,0:T(8,128)(2,1)} %wup.1) | copy-start | bytes 393220
  27.0 42.6 %copy-start.3 = (bf16[512,128]{1,0:T(8,128)(2,1)S(1)}, bf16[512,128]{1,0:T(8,128)(2,1)}, u32[]{:S(2)}) copy-start(bf16[512,128]{1,0:T(8,128)(2,1)} %wdown.1) | copy-start | bytes 393220
  27.0 42.6 %copy-start.10 = (s32[1,4096]{1,0:T(1,128)S(1)}, s32[1,4096]{1,0:T(1,128)}, u32[]{:S(2)}) copy-start(s32[1,4096]{1,0:T(1,128)} %hil.1) | copy-start | bytes 49156
  27.0 42.6 %copy-start.13 = (s32[1,128]{1,0:T(1,128)S(1)}, s32[1,128]{1,0:T(1,128)}, u32[]{:S(2)}) copy-start(s32[1,128]{1,0:T(1,128)} %cnt.1) | copy-start | bytes 1540
  27.0 42.6 %copy-start.14 = (f32[128]{0:T(128)S(1)}, f32[128]{0:T(128)}, u32[]{:S(2)}) copy-start(f32[128]{0:T(128)} %param.27) | copy-start | bytes 1540

commit v4 on v3

--- a/solution.py
+++ b/solution.py
@@ -317,103 +317,123 @@
     )(points.reshape(LA, LB, depth, C), occupied.reshape(1, rows), w_conv, cpe_proj, gain)
 
 
-def moved_kernel(cap, per, hil, cnt, mixed, gain, wup, wdown, out, starts, rowbuf, send, send_sem, recv_sem, own_sem):
+def moved_kernel(cap, per, hil, cnt, mixed, gain, wup, wdown, out, order, starts, rowbuf, send, send_sem, recv_sem, own_sem, order_sem, side_sem):
     n_x, n_y = lax.axis_size("gx"), lax.axis_size("gy")
     me_x, me_y = lax.axis_index("gx"), lax.axis_index("gy")
     me = me_x * n_y + me_y
     devices = n_x * n_y
-    last = hil.shape[1] - 1
-
-    def place(i):
-        return lax.rem(me_x + i // n_y, n_x), lax.rem(me_y + i % n_y, n_y)
-
+    rounds = devices // per
+    mesh_id = pl.DeviceIdType.MESH
+
+    def place(c, d):
+        return (me_x + d) & (n_x - 1), (me_y + (c + d * (n_y // n_x))) & (n_y - 1)
+
+    fetch = pltpu.make_async_copy(hil, order.at[:, pl.ds(0, hil.shape[1])], order_sem)
+    fetch.start()
     barrier = pltpu.get_barrier_semaphore()
-
-    def greet(i, carry):
-        pl.semaphore_signal(barrier, inc=1, device_id=place(i), device_id_type=pl.DeviceIdType.MESH)
-        return carry
-
-    lax.fori_loop(1, devices, greet, 0)
+    for d in range(1, n_y):
+        pl.semaphore_signal(barrier, inc=1, device_id=(me_x, (me_y + d) & (n_y - 1)), device_id_type=mesh_id)
+    for d in range(1, n_x):
+        pl.semaphore_signal(barrier, inc=1, device_id=((me_x + d) & (n_x - 1), me_y), device_id_type=mesh_id)
+
+    for j in range(cap):
+        order[0, hil.shape[1] + j] = 0
 
     def offset(e, total):
         starts[e] = total
         return total + cnt[0, e]
 
-    lax.fori_loop(0, devices, offset, jnp.int32(0))
-
-    def compute(c):
-        def rows_of(d, carry):
-            to_x, to_y = place(c * per + d)
+    lax.fori_loop(0, devices, offset, jnp.int32(0), unroll=8)
+    fetch.wait()
+
+    def collect(c, slot):
+        for d in range(per):
+            to_x, to_y = place(c, d)
             start = starts[to_x * n_y + to_y]
             for j in range(cap):
-                idx = hil[0, jnp.minimum(start + j, last)]
-                rowbuf[pl.ds(d * cap + j, 1), :] = mixed[pl.ds(idx, 1), :]
-            return carry
-
-        lax.fori_loop(0, per, rows_of, 0)
-        x = rowbuf[...]
+                idx = order[0, start + j]
+                rowbuf[slot, d * cap + j : d * cap + j + 1, :] = mixed[pl.ds(idx, 1), :]
+
+    def mlp(c, slot):
+        x = rowbuf[slot]
         mlp_in = norm_rows(x, gain[...]).astype(jnp.bfloat16)
         up = jnp.dot(mlp_in, wup[...], preferred_element_type=jnp.float32)
         hidden = jax.nn.gelu(up).astype(jnp.bfloat16)
         y = x + jnp.dot(hidden, wdown[...], preferred_element_type=jnp.float32)
-        slot = lax.broadcasted_iota(jnp.int32, (cap, C), 0)
+        row = lax.broadcasted_iota(jnp.int32, (cap, C), 0)
         for d in range(per):
-            to_x, to_y = place(c * per + d)
+            to_x, to_y = place(c, d)
             count = cnt[0, to_x * n_y + to_y]
-            send[c * per + d] = jnp.where(slot < count, y[d * cap : (d + 1) * cap], 0.0).astype(jnp.bfloat16)
-
-    def copy(i):
+            send[c * per + d] = jnp.where(row < count, y[d * cap : (d + 1) * cap], 0.0).astype(jnp.bfloat16)
+
+    def copy(c, d):
+        i = c * per + d
         return pltpu.make_async_remote_copy(
             src_ref=send.at[i],
             dst_ref=out.at[me],
             send_sem=send_sem.at[i],
             recv_sem=recv_sem.at[i],
-            device_id=place(i),
-            device_id_type=pl.DeviceIdType.MESH,
+            device_id=place(c, d),
+            device_id_type=mesh_id,
         )
 
-    def begin(i, carry):
-        copy(i).start()
-        return carry
-
-    compute(0)
+    collect(0, 0)
+    pl.semaphore_wait(barrier, n_x + n_y - 2)
+    for d in range(1, n_y):
+        pl.semaphore_signal(side_sem, inc=1, device_id=(me_x, (me_y + d) & (n_y - 1)), device_id_type=mesh_id)
+    collect(1, 1)
+    mlp(0, 0)
     own = pltpu.make_async_copy(send.at[0], out.at[me], own_sem)
     own.start()
-    pl.semaphore_wait(barrier, devices - 1)
-    lax.fori_loop(1, per, begin, 0)
-
-    def step(c, carry):
-        compute(c)
-        lax.fori_loop(c * per, (c + 1) * per, begin, 0)
-        return carry
-
-    lax.fori_loop(1, devices // per, step, 0)
+    pl.semaphore_wait(side_sem, n_y - 1)
+    for d in range(1, per):
+        copy(0, d).start()
+
+    def step(k, carry):
+        for u in range(2):
+            c = 2 * k + 1 + u
+            collect(c + 1, u)
+            mlp(c, 1 - u)
+            for d in range(per):
+                copy(c, d).start()
+        return carry
+
+    lax.fori_loop(0, rounds // 2 - 1, step, 0)
+    mlp(rounds - 1, 1)
+    for d in range(per):
+        copy(rounds - 1, d).start()
     own.wait()
-
-    def finish(i, carry):
-        copy(i).wait()
-        return carry
-
-    lax.fori_loop(1, devices, finish, 0)
+    for d in range(1, per):
+        copy(0, d).wait()
+
+    def finish(c, carry):
+        for d in range(per):
+            copy(c, d).wait()
+        return carry
+
+    lax.fori_loop(1, rounds, finish, 0)
 
 
 def move_rows(hilbert_order, send_counts, mixed, gain, w_up, w_down, cap):
     devices = send_counts.shape[1]
+    rows = hilbert_order.shape[1]
     per = 8
     vm = pl.BlockSpec(memory_space=pltpu.VMEM)
-    sm = pl.BlockSpec(memory_space=pltpu.SMEM)
     return pl.pallas_call(
         functools.partial(moved_kernel, cap, per),
         out_shape=jax.ShapeDtypeStruct((devices, cap, C), jnp.bfloat16),
-        in_specs=[sm, sm] + [vm] * 4,
+        in_specs=[pl.BlockSpec(memory_space=pl.ANY), pl.BlockSpec(memory_space=pltpu.SMEM)] + [vm] * 4,
         out_specs=pl.BlockSpec(memory_space=pl.ANY),
         scratch_shapes=[
+            pltpu.SMEM((1, rows + C), jnp.int32),
             pltpu.SMEM((devices,), jnp.int32),
-            pltpu.VMEM((per * cap, C), jnp.float32),
+            pltpu.VMEM((2, per * cap, C), jnp.float32),
             pltpu.VMEM((devices, cap, C), jnp.bfloat16),
             pltpu.SemaphoreType.DMA((devices,)),
             pltpu.SemaphoreType.DMA((devices,)),
             pltpu.SemaphoreType.DMA,
+            pltpu.SemaphoreType.DMA,
+            pltpu.SemaphoreType.REGULAR,
         ],
         compiler_params=pltpu.CompilerParams(
             vmem_limit_bytes=48 * 2**20, collective_id=1, has_side_effects=True

time: 108 us -> 100 us (0.926)
  Pallas kernels: 102 us -> 94.2 us
    pallas_call x1, Pallas kernels: 37.1 us -> 29.3 us  [move_rows(): pl.pallas_call(functools.partial(moved_kernel, cap, per), out_shape=jax.S...]
where the time goes in v4:
time: 100 us
  Pallas kernels  94.2 us (94%)
  local copies, waits for them, and re-layouts  5.64 us (6%)
    pallas_call x1, Pallas kernels, attention(): pl.pallas_call(attn_kernel, out_shape=jax.ShapeDtypeStruct((rows, C), jnp...  42.5 us
    pallas_call x1, Pallas kernels, move_rows(): pl.pallas_call(functools.partial(moved_kernel, cap, per), out_shape=jax.S...  29.3 us
    pallas_call x1, Pallas kernels, encode(): pl.pallas_call(encode_kernel, out_shape=jax.ShapeDtypeStruct((rows, C), j...  22.4 us
    unnamed x31, local copies, waits for them, and re-layouts  5.64 us

profile of v4, /device:TPU:1, one launch (start us, length us, event | category | flops | bytes accessed | tf_op | source)
XLA Modules:
  0.0 100.0 jit_solution(12328873793108631699)
XLA Ops:
  0.0 0.0 copy-start.12
  0.0 0.0 copy-start
  0.0 1.2 %copy-done = bf16[4096,128]{1,0:T(8,128)(2,1)S(1)} copy-done((bf16[4096,128]{1,0:T(8,128)(2,1)S(1)}, bf16[4096,128]{1,0:T(8,128)(2,1)}, u32[]{:S(2)}) %copy-start) | copy-done | bytes 1048600
  1.2 0.0 copy-start.1
  1.2 1.2 %copy-done.1 = bf16[27,128,128]{2,1,0:T(8,128)(2,1)S(1)} copy-done((bf16[27,128,128]{2,1,0:T(8,128)(2,1)S(1)}, bf16[27,128,128]{2,1,0:T(8,128)(2,1)}, u32[]{:S(2)}) %copy-start.1) | copy-done | bytes 884760
  2.4 0.0 copy-start.5
  2.4 0.8 copy-done.5
  3.2 0.0 copy-start.7
  3.2 0.7 copy-done.7
  3.9 0.0 copy-start.11
  3.9 0.7 copy-done.11
  4.5 0.0 copy-start.4
  4.5 0.0 copy-start.6
  4.5 0.0 copy-start.8
  4.5 0.0 copy-start.9
  4.6 22.4 %encode.1.res = f32[4096,128]{1,0:T(8,128)S(1)} custom-call(bf16[16,16,16,128]{3,2,1,0:T(8,128)(2,1)S(1)} %bitcast.7, s32[1,4096]{1,0:T(1,128)S(1)} %bitcast.8, bf16[27,128,128]{2,1,0:T(8,128)(2,1)S(1)} %copy-done.1, bf16[128,128]{1,0:T(8,128)(2,1)S(1)} %copy-done.5, f32[1,128]{1,0:T(1,128)S(1)} %bitcast.9), custom_call_target="tpu_custom_call" | custom-call | tf_op jit(solution)/shard_map/encode/pallas_call | solution.py:302
  26.9 0.0 copy-done.12
  27.0 0.0 copy-done.4
  27.0 0.0 copy-done.6
  27.0 0.0 copy-done.8
  27.0 0.0 copy-done.9
  27.0 0.0 copy-start.2
  27.0 0.0 copy-start.3
  27.0 0.0 copy-start.10
  27.0 0.0 copy-start.13
  27.0 0.0 copy-start.14
  27.1 42.5 %attention.1.mixed = f32[4096,128]{1,0:T(8,128)S(1)} custom-call(s32[1,4096]{1,0:T(1,128)S(1)} %copy-done.8, s32[1,4096]{1,0:T(1,128)S(1)} %copy-done.9, f32[4096,128]{1,0:T(8,128)S(1)} %encode.1.res, f32[1,128]{1,0:T(1,128)S(1)} %bitcast.10, bf16[128,384]{1,0:T(8,128)(2,1)S(1)} %copy-done.4, bf16[128,128]{1,0:T(8,128)(2,1)S(1)} %copy-done.6), custom_call_target="tpu_custom_call" | custom-call | tf_op jit(solution)/shard_map/attention/pallas_call | solution.py:140
  69.6 0.0 copy-done.2
  69.6 0.0 copy-done.3
  69.6 0.0 copy-done.10
  69.6 0.0 copy-done.13
  69.7 0.0 copy-done.14
  69.7 29.3 %move_rows.1 = bf16[128,40,128]{2,1,0:T(8,128)(2,1)S(1)} custom-call(s32[1,4096]{1,0:T(1,128)S(1)} %copy-done.10, s32[1,128]{1,0:T(1,128)S(1)} %copy-done.13, f32[4096,128]{1,0:T(8,128)S(1)} %attention.1.mixed, f32[1,128]{1,0:T(1,128)S(1)} %bitcast.11, bf16[128,512]{1,0:T(8,128)(2,1)S(1)} %copy-done.2, bf16[512,128]{1,0:T(8,128)(2,1)S(1)} %copy-done.3), custom_call_target="tpu_custom_call" | custom-call | tf_op jit(solution)/shard_map/move_rows/pallas_call | solution.py:422
  98.9 1.1 %copy.17 = bf16[5120,128]{1,0:T(8,128)(2,1)} copy(bf16[5120,128]{1,0:T(8,128)(2,1)S(1)} %bitcast.6) | data formatting | bytes 2621440
Async XLA Ops:
  0.0 26.9 %copy-start.12 = (f32[128]{0:T(128)S(1)}, f32[128]{0:T(128)}, u32[]{:S(2)}) copy-start(f32[128]{0:T(128)} %param.24) | copy-start | bytes 1540
  0.0 1.2 %copy-start = (bf16[4096,128]{1,0:T(8,128)(2,1)S(1)}, bf16[4096,128]{1,0:T(8,128)(2,1)}, u32[]{:S(2)}) copy-start(bf16[4096,128]{1,0:T(8,128)(2,1)} %param.15) | copy-start | bytes 3145732
  1.2 1.2 %copy-start.1 = (bf16[27,128,128]{2,1,0:T(8,128)(2,1)S(1)}, bf16[27,128,128]{2,1,0:T(8,128)(2,1)}, u32[]{:S(2)}) copy-start(bf16[27,128,128]{2,1,0:T(8,128)(2,1)} %wconv.1) | copy-start | bytes 2654212
  2.4 0.8 copy-start.5
  3.2 0.7 copy-start.7
  3.9 0.7 copy-start.11
  4.5 22.4 %copy-start.4 = (bf16[128,384]{1,0:T(8,128)(2,1)S(1)}, bf16[128,384]{1,0:T(8,128)(2,1)}, u32[]{:S(2)}) copy-start(bf16[128,384]{1,0:T(8,128)(2,1)} %wqkv.1) | copy-start | bytes 294916
  4.5 22.4 %copy-start.6 = (bf16[128,128]{1,0:T(8,128)(2,1)S(1)}, bf16[128,128]{1,0:T(8,128)(2,1)}, u32[]{:S(2)}) copy-start(bf16[128,128]{1,0:T(8,128)(2,1)} %wout.1) | copy-start | bytes 98308
  4.5 22.4 %copy-start.8 = (s32[1,4096]{1,0:T(1,128)S(1)}, s32[1,4096]{1,0:T(1,128)}, u32[]{:S(2)}) copy-start(s32[1,4096]{1,0:T(1,128)} %zord.1) | copy-start | bytes 49156
  4.5 22.4 %copy-start.9 = (s32[1,4096]{1,0:T(1,128)S(1)}, s32[1,4096]{1,0:T(1,128)}, u32[]{:S(2)}) copy-start(s32[1,4096]{1,0:T(1,128)} %pad.1) | copy-start | bytes 49156
  27.0 42.6 %copy-start.2 = (bf16[128,512]{1,0:T(8,128)(2,1)S(1)}, bf16[128,512]{1,0:T(8,128)(2,1)}, u32[]{:S(2)}) copy-start(bf16[128,512]{1,0:T(8,128)(2,1)} %wup.1) | copy-start | bytes 393220
  27.0 42.6 %copy-start.3 = (bf16[512,128]{1,0:T(8,128)(2,1)S(1)}, bf16[512,128]{1,0:T(8,128)(2,1)}, u32[]{:S(2)}) copy-start(bf16[512,128]{1,0:T(8,128)(2,1)} %wdown.1) | copy-start | bytes 393220
  27.0 42.6 %copy-start.10 = (s32[1,4096]{1,0:T(1,128)S(1)}, s32[1,4096]{1,0:T(1,128)}, u32[]{:S(2)}) copy-start(s32[1,4096]{1,0:T(1,128)} %hil.1) | copy-start | bytes 49156
  27.0 42.6 %copy-start.13 = (s32[1,128]{1,0:T(1,128)S(1)}, s32[1,128]{1,0:T(1,128)}, u32[]{:S(2)}) copy-start(s32[1,128]{1,0:T(1,128)} %cnt.1) | copy-start | bytes 1540
  27.0 42.6 %copy-start.14 = (f32[128]{0:T(128)S(1)}, f32[128]{0:T(128)}, u32[]{:S(2)}) copy-start(f32[128]{0:T(128)} %param.27) | copy-start | bytes 1540

commit v5 on v2

v5 whole, which is shorter than its diff:
```python
import functools
import math
import types
import jax
import jax.numpy as jnp
from jax import lax
from jax.experimental import pallas as pl
from jax.experimental.pallas import tpu as pltpu
from jax.sharding import PartitionSpec as P

C = 128
LA = 16
LB = 16
HEADS = 8
PATCH = 1024
HEAD_DIM = 16
QB = 256
UNROLL = 2


def norm_rows(v, gain):
    center = v - jnp.mean(v, axis=-1, keepdims=True)
    spread = jnp.mean(center * center, axis=-1, keepdims=True)
    return center * lax.rsqrt(spread + 1e-05) * gain


LOADS = (
    "pts",
    "occ",
    "order_z",
    "pad",
    "order",
    "cnt",
    "wconv",
    "proj",
    "cgain",
    "again",
    "wqkv",
    "wout",
    "mgain",
    "wup",
    "wdown",
)


def block_kernel(cap, per, names, *refs):
    r = types.SimpleNamespace(**dict(zip(names, refs)))
    rows = r.residual.shape[0]
    loads = {}
    for k, name in enumerate(LOADS):
        source, goal = getattr(r, name + "_in"), getattr(r, name)
        if name == "order":
            goal = goal.at[:, pl.ds(0, rows)]
        loads[name] = pltpu.make_async_copy(source, goal, r.load_sem.at[k])
    for load in loads.values():
        load.start()

    def wait_for(*wanted):
        for name in wanted:
            loads[name].wait()

    encode(r, wait_for)
    attend(r, wait_for)
    move(r, wait_for, cap, per)


def prepare(r):
    qw, vt = r.qw, r.vt
    half = C // 2
    first = lax.broadcasted_iota(jnp.int32, (HEAD_DIM, PATCH), 0) == 0
    unit = jnp.where(first, 1.0, 0.0).astype(jnp.bfloat16)
    for h in range(HEADS):
        qw[h] = jnp.zeros((2 * C, PATCH), jnp.bfloat16)
        qw[h, 3 * half : 3 * half + HEAD_DIM] = unit
        vt[h, HEAD_DIM:] = unit


def encode(r, wait_for):
    pts, occ, wconv, proj, cgain = r.pts, r.occ, r.wconv, r.proj, r.cgain
    residual, win, taps = r.residual, r.win, r.taps
    halo_send, halo_recv, side_sem = r.halo_send, r.halo_recv, r.side_sem
    n_x, n_y = lax.axis_size("gx"), lax.axis_size("gy")
    me_x, me_y = lax.axis_index("gx"), lax.axis_index("gy")
    z = pts.shape[2]
    cols = C // z
    sides = [(dx, dy) for dx in (-1, 0, 1) for dy in (-1, 0, 1) if (dx, dy) != (0, 0)]

    def place(dx, dy):
        return lax.rem(me_x + (dx + n_x), n_x), lax.rem(me_y + (dy + n_y), n_y)

    barrier = pltpu.get_barrier_semaphore()
    row = [((me_x + d) & (n_x - 1), me_y) for d in range(1, n_x)]
    col = [(me_x, (me_y + d) & (n_y - 1)) for d in range(1, n_y)]
    met = row + col + [place(dx, dy) for dx, dy in sides if dx and dy]
    for device in met:
        pl.semaphore_signal(barrier, inc=1, device_id=device, device_id_type=pl.DeviceIdType.MESH)

    rr = lax.broadcasted_iota(jnp.int32, (C, C), 0)
    cc = lax.broadcasted_iota(jnp.int32, (C, C), 1)

    def pick(dz, row):
        hit = (cc == rr + dz) & (rr // z == cc // z)
        return jnp.where(hit, row, 0.0).astype(jnp.bfloat16)

    def put(dz, a, b, block):
        win[dz + 1, a, b] = block.astype(jnp.bfloat16).reshape(block.shape[0] // z, z, C)

    def own_block(r):
        a, b = r // 2, lax.rem(r, 2) * cols
        row = jnp.where(occ[:, pl.ds(pl.multiple_of(r * C, C), C)] > 0, 1.0, 0.0)
        return a, b, row, pts[a, pl.ds(b, cols)].reshape(C, C)

    wait_for("pts", "occ")

    def fill(r, carry):
        a, b, row, block = own_block(r)
        put(0, a + 1, pl.ds(b + 1, cols), jnp.dot(pick(0, row), block, preferred_element_type=jnp.float32))
        return carry

    lax.fori_loop(0, LA * LB // cols, fill, 0, unroll=8)

    def span(d, n):
        here = {-1: pl.ds(1, 1), 0: pl.ds(1, n), 1: pl.ds(n, 1)}[d]
        there = {-1: pl.ds(n + 1, 1), 0: pl.ds(1, n), 1: pl.ds(0, 1)}[d]
        return here, there

    copies = []
    for k, (dx, dy) in enumerate(sides):
        (from_a, to_a), (from_b, to_b) = span(dx, LA), span(dy, LB)
        copies.append(
            pltpu.make_async_remote_copy(
                src_ref=win.at[1, from_a, from_b],
                dst_ref=win.at[1, to_a, to_b],
                send_sem=halo_send.at[k],
                recv_sem=halo_recv.at[k],
                device_id=place(dx, dy),
                device_id_type=pl.DeviceIdType.MESH,
            )
        )
    pl.semaphore_wait(barrier, len(met))
    for copy in copies:
        copy.start()
    for device in col:
        pl.semaphore_signal(side_sem, inc=1, device_id=device, device_id_type=pl.DeviceIdType.MESH)

    def shift(r, carry):
        a, b, row, block = own_block(r)
        for dz in (-1, 1):
            put(dz, a + 1, pl.ds(b + 1, cols), jnp.dot(pick(dz, row), block, preferred_element_type=jnp.float32))
        return carry

    lax.fori_loop(0, LA * LB // cols, shift, 0, unroll=4)
    wait_for("wconv", "proj", "cgain")
    prepare(r)

    none = jnp.zeros((C, C), jnp.bfloat16)
    for i in range(4):
        for sb in range(3):
            for sz in range(3):
                at = ((i * 3 + sb) * 3 + sz) * C
                taps[at : at + C, :C] = wconv[i * 9 + sb * 3 + sz] if i < 3 else none
                taps[at : at + C, C:] = wconv[(i - 1) * 9 + sb * 3 + sz] if i > 0 else none

    for copy in copies:
        copy.wait()

    low_x = jnp.where(me_x > 0, 1.0, 0.0)
    high_x = jnp.where(me_x < n_x - 1, 1.0, 0.0)
    low_y = jnp.where(me_y > 0, 1.0, 0.0)
    high_y = jnp.where(me_y < n_y - 1, 1.0, 0.0)

    def edge(a, b, count, live):
        block = win[1, a, b].reshape(count * z, C)
        for dz in (-1, 0, 1):
            mat = pick(dz, live)[: count * z, : count * z]
            put(dz, a, b, jnp.dot(mat, block, preferred_element_type=jnp.float32))

    for half in range(2):
        run = pl.ds(1 + half * cols, cols)
        edge(0, run, cols, low_x)
        edge(LA + 1, run, cols, high_x)
        edge(run, 0, cols, low_y)
        edge(run, LB + 1, cols, high_y)
    for a, live_x in ((0, low_x), (LA + 1, high_x)):
        for b, live_y in ((0, low_y), (LB + 1, high_y)):
            edge(a, pl.ds(b, 1), 1, live_x * live_y)

    tall = 2
    wide = LB * z

    def conv(t):
        total = None
        for sb in range(3):
            for pair in range(2):
                pieces = []
                for i in (2 * pair, 2 * pair + 1):
                    for sz in range(3):
                        pieces.append(
                            jnp.concatenate(
                                [
                                    win[sz, (t * tall + u) * 2 + i, sb : sb + LB].reshape(wide, C)
                                    for u in range(tall)
                                ],
                                axis=0,
                            )
                        )
                w = jnp.concatenate(
                    [taps[((i * 3 + sb) * 3) * C : ((i * 3 + sb) * 3 + 3) * C, :] for i in (2 * pair, 2 * pair + 1)],
                    axis=0,
                )
                term = jnp.dot(jnp.concatenate(pieces, axis=1), w, preferred_element_type=jnp.float32)
                total = term if total is None else total + term
        for o in range(2):
            conv_out = total[:, o * C : (o + 1) * C].astype(jnp.bfloat16)
            encoded = norm_rows(
                jnp.dot(conv_out, proj[...], preferred_element_type=jnp.float32), cgain[...]
            )
            for u in range(tall):
                a = (t * tall + u) * 2 + o
                residual[a * wide : (a + 1) * wide, :] = (
                    pts[a].reshape(wide, C).astype(jnp.float32) + encoded[u * wide : (u + 1) * wide]
                )

    for t in range(LA // 2 // tall):
        conv(t)


def attend(r, wait_for):
    order_z, pad, again, wqkv, wout = r.order_z, r.pad, r.again, r.wqkv, r.wout
    residual, mixed, serial = r.residual, r.mixed, r.serial
    qw, ka, vt = r.qw, r.ka, r.vt
    heads, live, bd, sbuf = r.heads, r.live, r.bd, r.sbuf
    rows = serial.shape[0]
    blocks = PATCH // QB
    half = C // 2

    def gather(i, carry):
        base = i * 16
        for u in range(16):
            idx = order_z[0, base + u]
            serial[pl.ds(base + u, 1), :] = residual[pl.ds(idx, 1), :]
        return carry

    wait_for("order_z")
    lax.fori_loop(0, rows // 16, gather, 0)
    wait_for("pad", "again", "wqkv", "wout")

    def patch(p, carry):
        off = pl.multiple_of(p * PATCH, PATCH)
        attn_in = norm_rows(serial[pl.ds(off, PATCH), :], again[...]).astype(jnp.bfloat16)
        proj = jnp.dot(attn_in, wqkv[...], preferred_element_type=jnp.float32)
        proj = proj.astype(jnp.bfloat16).astype(jnp.float32)
        qt = proj[:, :C].T * jnp.float32(HEAD_DIM ** -0.5 * math.log2(math.e))
        high = qt.astype(jnp.bfloat16)
        rest = qt - high.astype(jnp.float32)
        mid = rest.astype(jnp.bfloat16)
        low = (rest - mid.astype(jnp.float32)).astype(jnp.bfloat16)
        vals = proj[:, 2 * C :].T.astype(jnp.bfloat16)
        for h in range(HEADS):
            sl = slice(h * HEAD_DIM, (h + 1) * HEAD_DIM)
            at = h % 4 * HEAD_DIM
            qw[h, at : at + HEAD_DIM] = high[sl]
            qw[h, half + at : half + at + HEAD_DIM] = mid[sl]
            qw[h, C + at : C + at + HEAD_DIM] = low[sl]
            vt[h, :HEAD_DIM] = vals[sl]
        rr = lax.broadcasted_iota(jnp.int32, (C, C), 0)
        cc = lax.broadcasted_iota(jnp.int32, (C, C), 1)
        real = jnp.where(pad[:, pl.ds(off, PATCH)] > 0, 1.0, 0.0)
        for b in range(PATCH // C):
            diag = jnp.where(rr == cc, real[:, b * C : (b + 1) * C], 0.0).astype(jnp.bfloat16)
            live[b * C : (b + 1) * C] = jnp.dot(
                diag, jnp.ones((C, C), jnp.bfloat16), preferred_element_type=jnp.float32
            )
        bias = (1.0 - live[...]) * -1e30
        k = proj[:, C : 2 * C]
        kr = pltpu.roll(k, half, 1)
        left = lax.broadcasted_iota(jnp.int32, (PATCH, C), 1) < half
        ka[0, :, :C] = jnp.where(left, k, kr).astype(jnp.bfloat16)
        ka[0, :, C:] = jnp.where(left, k, bias).astype(jnp.bfloat16)
        ka[1, :, :C] = jnp.where(left, kr, k).astype(jnp.bfloat16)
        ka[1, :, C:] = jnp.where(left, kr, bias).astype(jnp.bfloat16)
        rr = lax.broadcasted_iota(jnp.int32, (QB, QB), 0)
        cc = lax.broadcasted_iota(jnp.int32, (QB, QB), 1)
        for b in range(blocks):
            col = bias[b * QB : (b + 1) * QB]
            bd[b] = jnp.where(rr == cc, 0.0, jnp.concatenate([col, col], axis=1))

        def scores(h, b, t):
            g = h // 4
            qs = slice(b * QB, (b + 1) * QB)
            ts = slice(t * QB, (t + 1) * QB)
            if t == b:
                w = jnp.concatenate(
                    [qw[h, : 3 * half, qs], jnp.zeros((half, QB), jnp.bfloat16)], axis=0
                )
                s = jnp.dot(ka[g, ts], w, preferred_element_type=jnp.float32) + bd[b]
            else:
                s = jnp.dot(ka[g, ts], qw[h, :, qs], preferred_element_type=jnp.float32)
            sbuf[b % 2, ts] = s
            return jnp.max(s.reshape(QB // 8, 8, QB), axis=0)

        def values(h, b, t, peak):
            ts = slice(t * QB, (t + 1) * QB)
            prob = jnp.exp2(sbuf[b % 2, ts] - peak).astype(jnp.bfloat16)
            return jnp.dot(vt[h, :, ts], prob, preferred_element_type=jnp.float32)

        def top(parts):
            m = functools.reduce(jnp.maximum, parts)
            return jnp.max(m, axis=0, keepdims=True)

        start = top([scores(0, 0, t) for t in range(blocks)])

        def head(h, peak):
            for b in range(blocks):
                h2, b2 = (h, b + 1) if b + 1 < blocks else (lax.rem(h + 1, HEADS), 0)
                parts = []
                total = None
                for t in range(blocks):
                    parts.append(scores(h2, b2, t))
                    term = values(h, b, t, peak)
                    total = term if total is None else total + term
                heads[pl.ds(pl.multiple_of(h * HEAD_DIM, HEAD_DIM), HEAD_DIM), b * QB : (b + 1) * QB] = (
                    total[:HEAD_DIM] / total[HEAD_DIM : HEAD_DIM + 1]
                )
                peak = top(parts)
            return peak

        lax.fori_loop(0, HEADS, head, start, unroll=UNROLL)
        mixed_heads = heads[...].T.astype(jnp.bfloat16)
        part = jnp.dot(mixed_heads, wout[...], preferred_element_type=jnp.float32)
        at = pl.ds(off, PATCH)
        mixed[at, :] = serial[at, :] + live[...] * part
        return carry

    lax.fori_loop(0, rows // PATCH, patch, 0)


def move(r, wait_for, cap, per):
    out, mixed, order, cnt = r.out, r.mixed, r.order, r.cnt
    mgain, wup, wdown = r.mgain, r.wup, r.wdown
    starts, rowbuf, send = r.starts, r.rowbuf, r.send
    send_sem, recv_sem, own_sem, side_sem = r.send_sem, r.recv_sem, r.own_sem, r.side_sem
    n_x, n_y = lax.axis_size("gx"), lax.axis_size("gy")
    me_x, me_y = lax.axis_index("gx"), lax.axis_index("gy")
    rows = mixed.shape[0]
    me = me_x * n_y + me_y
    devices = n_x * n_y
    rounds = devices // per
    mesh_id = pl.DeviceIdType.MESH

    def target(c, d):
        return (me_x + d) & (n_x - 1), (me_y + (c + d * (n_y // n_x))) & (n_y - 1)

    for j in range(cap):
        order[0, rows + j] = 0

    wait_for("order", "cnt", "mgain", "wup", "wdown")

    def offset(e, total):
        starts[e] = total
        return total + cnt[0, e]

    lax.fori_loop(0, devices, offset, jnp.int32(0), unroll=8)

    def collect(c, slot):
        for d in range(per):
            to_x, to_y = target(c, d)
            start = starts[to_x * n_y + to_y]
            for j in range(cap):
                idx = order[0, start + j]
                rowbuf[slot, d * cap + j : d * cap + j + 1, :] = mixed[pl.ds(idx, 1), :]

    def mlp(c, slot):
        x = rowbuf[slot]
        mlp_in = norm_rows(x, mgain[...]).astype(jnp.bfloat16)
        up = jnp.dot(mlp_in, wup[...], preferred_element_type=jnp.float32)
        hidden = jax.nn.gelu(up).astype(jnp.bfloat16)
        y = x + jnp.dot(hidden, wdown[...], preferred_element_type=jnp.float32)
        row = lax.broadcasted_iota(jnp.int32, (cap, C), 0)
        for d in range(per):
            to_x, to_y = target(c, d)
            count = cnt[0, to_x * n_y + to_y]
            send[c * per + d] = jnp.where(row < count, y[d * cap : (d + 1) * cap], 0.0).astype(jnp.bfloat16)

    def copy(c, d):
        i = c * per + d
        return pltpu.make_async_remote_copy(
            src_ref=send.at[i],
            dst_ref=out.at[me],
            send_sem=send_sem.at[i],
            recv_sem=recv_sem.at[i],
            device_id=target(c, d),
            device_id_type=mesh_id,
        )

    collect(0, 0)
    collect(1, 1)
    mlp(0, 0)
    own = pltpu.make_async_copy(send.at[0], out.at[me], own_sem)
    own.start()
    pl.semaphore_wait(side_sem, n_y - 1)
    for d in range(1, per):
        copy(0, d).start()

    def step(k, carry):
        for u in range(2):
            c = 2 * k + 1 + u
            collect(c + 1, u)
            mlp(c, 1 - u)
            for d in range(per):
                copy(c, d).start()
        return carry

    lax.fori_loop(0, rounds // 2 - 1, step, 0)
    mlp(rounds - 1, 1)
    for d in range(per):
        copy(rounds - 1, d).start()
    own.wait()
    for d in range(1, per):
        copy(0, d).wait()

    def finish(c, carry):
        for d in range(per):
            copy(c, d).wait()
        return carry

    lax.fori_loop(1, rounds, finish, 0)


def body(
    points,
    occupied,
    z_order,
    pad_mask,
    hilbert_order,
    send_counts,
    w_conv,
    cpe_proj,
    cpe_gain,
    attn_gain,
    w_qkv,
    w_out,
    mlp_gain,
    w_up,
    w_down,
):
    rows = points.shape[0]
    depth = rows // (LA * LB)
    devices = lax.axis_size("gx") * lax.axis_size("gy")
    cap = rows // devices + max(2, rows // (4 * devices))
    per = lax.axis_size("gx")
    operands = {
        "pts": points.reshape(LA, LB, depth, C),
        "occ": occupied.reshape(1, rows),
        "order_z": z_order,
        "pad": pad_mask,
        "order": hilbert_order,
        "cnt": send_counts,
        "wconv": w_conv,
        "proj": cpe_proj,
        "cgain": cpe_gain.reshape(1, C),
        "again": attn_gain.reshape(1, C),
        "wqkv": w_qkv,
        "wout": w_out,
        "mgain": mlp_gain.reshape(1, C),
        "wup": w_up,
        "wdown": w_down,
    }
    scratch = {}
    for name, array in operands.items():
        scalar = name in ("order_z", "order", "cnt")
        shape = (1, rows + C) if name == "order" else array.shape
        scratch[name] = (pltpu.SMEM if scalar else pltpu.VMEM)(shape, array.dtype)
    f32, bf16 = jnp.float32, jnp.bfloat16
    dma = pltpu.SemaphoreType.DMA
    scratch.update(
        residual=pltpu.VMEM((rows, C), f32),
        mixed=pltpu.VMEM((rows, C), f32),
        serial=pltpu.VMEM((rows, C), f32),
        win=pltpu.VMEM((3, LA + 2, LB + 2, depth, C), bf16),
        taps=pltpu.VMEM((36 * C, 2 * C), bf16),
        qw=pltpu.VMEM((HEADS, 2 * C, PATCH), bf16),
        ka=pltpu.VMEM((2, PATCH, 2 * C), bf16),
        vt=pltpu.VMEM((HEADS, 2 * HEAD_DIM, PATCH), bf16),
        heads=pltpu.VMEM((C, PATCH), f32),
        live=pltpu.VMEM((PATCH, C), f32),
        bd=pltpu.VMEM((PATCH // QB, QB, QB), f32),
        sbuf=pltpu.VMEM((2, PATCH, QB), f32),
        starts=pltpu.SMEM((devices,), jnp.int32),
        rowbuf=pltpu.VMEM((2, per * cap, C), f32),
        send=pltpu.VMEM((devices, cap, C), bf16),
        load_sem=dma((len(LOADS),)),
        halo_send=dma((8,)),
        halo_recv=dma((8,)),
        send_sem=dma((devices,)),
        recv_sem=dma((devices,)),
        own_sem=dma,
        side_sem=pltpu.SemaphoreType.REGULAR,
    )
    names = [name + "_in" for name in LOADS] + ["out"] + list(scratch)
    moved = pl.pallas_call(
        functools.partial(block_kernel, cap, per, names),
        out_shape=jax.ShapeDtypeStruct((devices, cap, C), bf16),
        in_specs=[pl.BlockSpec(memory_space=pltpu.HBM)] * len(LOADS),
        out_specs=pl.BlockSpec(memory_space=pltpu.HBM),
        scratch_shapes=list(scratch.values()),
        compiler_params=pltpu.CompilerParams(
            vmem_limit_bytes=62 * 2**20, collective_id=0, has_side_effects=True
        ),
        name="block",
    )(*[operands[name] for name in LOADS])
    return moved.reshape(devices * cap, C)


def solution(mesh):
    placed = (
        P(("gx", "gy"), None),
        P(("gx", "gy")),
        P(("gx", "gy"), None),
        P(("gx", "gy"), None),
        P(("gx", "gy"), None),
        P(("gx", "gy"), None),
        P(),
        P(),
        P(),
        P(),
        P(),
        P(),
        P(),
        P(),
        P(),
    )
    return jax.shard_map(
        body, mesh=mesh, in_specs=placed, out_specs=P(("gx", "gy"), None), check_vma=False
    )
```

time: 127 us -> 91.4 us (0.72)
  Pallas kernels: 121 us -> 88.8 us
  local copies, waits for them, and re-layouts: 5.64 us -> 2.46 us
    pallas_call x3 -> x1, Pallas kernels: 121 us -> 88.8 us  [body(): pl.pallas_call(functools.partial(block_kernel, cap, per, names), out_shap...]
    unnamed x31 -> x1, local copies, waits for them, and re-layouts: 5.64 us -> 2.46 us
where the time goes in v5:
time: 91.4 us; the launch traced here: 91.2 us
  Pallas kernels  88.8 us (97%)
  local copies, waits for them, and re-layouts  2.46 us (3%)
    pallas_call x1, Pallas kernels, body(): pl.pallas_call(functools.partial(block_kernel, cap, per, names), out_shap...  88.8 us
    unnamed x1, local copies, waits for them, and re-layouts  2.46 us

profile of v5, /device:TPU:1, one launch (start us, length us, event | category | flops | bytes accessed | tf_op | source)
XLA Modules:
  0.0 91.2 jit_solution(16319658982082384145)
XLA Ops:
  0.0 88.8 %block.1 = bf16[128,40,128]{2,1,0:T(8,128)(2,1)} custom-call(bf16[16,16,16,128]{3,2,1,0:T(8,128)(2,1)} %bitcast.7, s32[1,4096]{1,0:T(1,128)} %bitcast.8, s32[1,4096]{1,0:T(1,128)} %refs_2_.1, s32[1,4096]{1,0:T(1,128)} %refs_3_.1, s32[1,4096]{1,0:T(1,128)} %refs_4_.1, s32[1,128]{1,0:T(1,128)} %refs_5_.1, bf16[27,128,128]{2,1,0:T(8,128)(2,1)} %refs_6_.1, ...), custom_call_target="tpu_custom_call" | custom-call | tf_op jit(solution)/shard_map/block/pallas_call | solution.py:501
  88.8 2.5 %copy.17 = bf16[5120,128]{1,0:T(8,128)(2,1)} copy(bf16[5120,128]{1,0:T(8,128)(2,1)} %bitcast.6) | data formatting | bytes 2621440

commit v6 on v5

--- a/solution.py
+++ b/solution.py
@@ -15,6 +15,7 @@
 PATCH = 1024
 HEAD_DIM = 16
 QB = 256
+KB = 512
 UNROLL = 2
 
 
@@ -75,6 +76,20 @@
         vt[h, HEAD_DIM:] = unit
 
 
+def offsets(r):
+    order, cnt, starts = r.order, r.cnt, r.starts
+    rows = order.shape[1] - C
+    devices = starts.shape[0]
+    for j in range(C):
+        order[0, rows + j] = 0
+
+    def offset(e, total):
+        starts[e] = total
+        return total + cnt[0, e]
+
+    lax.fori_loop(0, devices, offset, jnp.int32(0), unroll=8)
+
+
 def encode(r, wait_for):
     pts, occ, wconv, proj, cgain = r.pts, r.occ, r.wconv, r.proj, r.cgain
     residual, win, taps = r.residual, r.win, r.taps
@@ -137,6 +152,8 @@
                 device_id_type=pl.DeviceIdType.MESH,
             )
         )
+    wait_for("order", "cnt")
+    offsets(r)
     pl.semaphore_wait(barrier, len(met))
     for copy in copies:
         copy.start()
@@ -229,33 +246,36 @@
     order_z, pad, again, wqkv, wout = r.order_z, r.pad, r.again, r.wqkv, r.wout
     residual, mixed, serial = r.residual, r.mixed, r.serial
     qw, ka, vt = r.qw, r.ka, r.vt
-    heads, live, bd, sbuf = r.heads, r.live, r.bd, r.sbuf
+    heads, live, own, sbuf = r.heads, r.live, r.own, r.sbuf
     rows = serial.shape[0]
     blocks = PATCH // QB
     half = C // 2
 
-    def gather(i, carry):
-        base = i * 16
-        for u in range(16):
+    def gather(base, count):
+        for u in range(count):
             idx = order_z[0, base + u]
             serial[pl.ds(base + u, 1), :] = residual[pl.ds(idx, 1), :]
+
+    def gather_some(i, carry):
+        gather(i * 16, 16)
         return carry
 
     wait_for("order_z")
-    lax.fori_loop(0, rows // 16, gather, 0)
+    lax.fori_loop(0, PATCH // 16, gather_some, 0)
     wait_for("pad", "again", "wqkv", "wout")
 
     def patch(p, carry):
         off = pl.multiple_of(p * PATCH, PATCH)
         attn_in = norm_rows(serial[pl.ds(off, PATCH), :], again[...]).astype(jnp.bfloat16)
         proj = jnp.dot(attn_in, wqkv[...], preferred_element_type=jnp.float32)
-        proj = proj.astype(jnp.bfloat16).astype(jnp.float32)
-        qt = proj[:, :C].T * jnp.float32(HEAD_DIM ** -0.5 * math.log2(math.e))
+        proj = proj.astype(jnp.bfloat16)
+        turned = proj.T
+        qt = turned[:C].astype(jnp.float32) * jnp.float32(HEAD_DIM ** -0.5 * math.log2(math.e))
         high = qt.astype(jnp.bfloat16)
         rest = qt - high.astype(jnp.float32)
         mid = rest.astype(jnp.bfloat16)
         low = (rest - mid.astype(jnp.float32)).astype(jnp.bfloat16)
-        vals = proj[:, 2 * C :].T.astype(jnp.bfloat16)
+        vals = turned[2 * C :]
         for h in range(HEADS):
             sl = slice(h * HEAD_DIM, (h + 1) * HEAD_DIM)
             at = h % 4 * HEAD_DIM
@@ -272,35 +292,35 @@
                 diag, jnp.ones((C, C), jnp.bfloat16), preferred_element_type=jnp.float32
             )
         bias = (1.0 - live[...]) * -1e30
-        k = proj[:, C : 2 * C]
+        k = proj[:, C : 2 * C].astype(jnp.float32)
         kr = pltpu.roll(k, half, 1)
         left = lax.broadcasted_iota(jnp.int32, (PATCH, C), 1) < half
         ka[0, :, :C] = jnp.where(left, k, kr).astype(jnp.bfloat16)
         ka[0, :, C:] = jnp.where(left, k, bias).astype(jnp.bfloat16)
         ka[1, :, :C] = jnp.where(left, kr, k).astype(jnp.bfloat16)
         ka[1, :, C:] = jnp.where(left, kr, bias).astype(jnp.bfloat16)
+        keyed = qt * turned[C : 2 * C].astype(jnp.float32)
+        own[...] = jnp.sum(keyed.reshape(HEADS, HEAD_DIM, PATCH), axis=1, keepdims=True)
         rr = lax.broadcasted_iota(jnp.int32, (QB, QB), 0)
         cc = lax.broadcasted_iota(jnp.int32, (QB, QB), 1)
-        for b in range(blocks):
-            col = bias[b * QB : (b + 1) * QB]
-            bd[b] = jnp.where(rr == cc, 0.0, jnp.concatenate([col, col], axis=1))
 
         def scores(h, b, t):
-            g = h // 4
             qs = slice(b * QB, (b + 1) * QB)
-            ts = slice(t * QB, (t + 1) * QB)
-            if t == b:
-                w = jnp.concatenate(
-                    [qw[h, : 3 * half, qs], jnp.zeros((half, QB), jnp.bfloat16)], axis=0
-                )
-                s = jnp.dot(ka[g, ts], w, preferred_element_type=jnp.float32) + bd[b]
-            else:
-                s = jnp.dot(ka[g, ts], qw[h, :, qs], preferred_element_type=jnp.float32)
-            sbuf[b % 2, ts] = s
-            return jnp.max(s.reshape(QB // 8, 8, QB), axis=0)
+            s = jnp.dot(
+                ka[h // 4, t * KB : (t + 1) * KB], qw[h, :, qs], preferred_element_type=jnp.float32
+            )
+            pieces = [s[i * QB : (i + 1) * QB] for i in range(KB // QB)]
+            same = b - t * (KB // QB)
+            if 0 <= same < len(pieces):
+                pieces[same] = jnp.where(rr == cc, own[h, :, qs], pieces[same])
+            tops = []
+            for i, piece in enumerate(pieces):
+                sbuf[b % 2, t * KB + i * QB : t * KB + (i + 1) * QB] = piece
+                tops.append(jnp.max(piece.reshape(QB // 8, 8, QB), axis=0))
+            return functools.reduce(jnp.maximum, tops)
 
         def values(h, b, t, peak):
-            ts = slice(t * QB, (t + 1) * QB)
+            ts = slice(t * KB, (t + 1) * KB)
             prob = jnp.exp2(sbuf[b % 2, ts] - peak).astype(jnp.bfloat16)
             return jnp.dot(vt[h, :, ts], prob, preferred_element_type=jnp.float32)
 
@@ -308,14 +328,16 @@
             m = functools.reduce(jnp.maximum, parts)
             return jnp.max(m, axis=0, keepdims=True)
 
-        start = top([scores(0, 0, t) for t in range(blocks)])
+        start = top([scores(0, 0, t) for t in range(PATCH // KB)])
 
         def head(h, peak):
+            share = PATCH // HEADS
+            gather(pl.multiple_of(lax.rem(p + 1, rows // PATCH) * PATCH + h * share, share), share)
             for b in range(blocks):
                 h2, b2 = (h, b + 1) if b + 1 < blocks else (lax.rem(h + 1, HEADS), 0)
                 parts = []
                 total = None
-                for t in range(blocks):
+                for t in range(PATCH // KB):
                     parts.append(scores(h2, b2, t))
                     term = values(h, b, t, peak)
                     total = term if total is None else total + term
@@ -326,7 +348,7 @@
             return peak
 
         lax.fori_loop(0, HEADS, head, start, unroll=UNROLL)
-        mixed_heads = heads[...].T.astype(jnp.bfloat16)
+        mixed_heads = heads[...].astype(jnp.bfloat16).T
         part = jnp.dot(mixed_heads, wout[...], preferred_element_type=jnp.float32)
         at = pl.ds(off, PATCH)
         mixed[at, :] = serial[at, :] + live[...] * part
@@ -349,18 +371,9 @@
     mesh_id = pl.DeviceIdType.MESH
 
     def target(c, d):
-        return (me_x + d) & (n_x - 1), (me_y + (c + d * (n_y // n_x))) & (n_y - 1)
-
-    for j in range(cap):
-        order[0, rows + j] = 0
-
-    wait_for("order", "cnt", "mgain", "wup", "wdown")
-
-    def offset(e, total):
-        starts[e] = total
-        return total + cnt[0, e]
-
-    lax.fori_loop(0, devices, offset, jnp.int32(0), unroll=8)
+        return me_x ^ d, me_y ^ (c ^ (d * (n_y // n_x)))
+
+    wait_for("mgain", "wup", "wdown")
 
     def collect(c, slot):
         for d in range(per):
@@ -394,13 +407,13 @@
         )
 
     collect(0, 0)
-    collect(1, 1)
     mlp(0, 0)
     own = pltpu.make_async_copy(send.at[0], out.at[me], own_sem)
     own.start()
     pl.semaphore_wait(side_sem, n_y - 1)
     for d in range(1, per):
         copy(0, d).start()
+    collect(1, 1)
 
     def step(k, carry):
         for u in range(2):
@@ -484,7 +497,7 @@
         vt=pltpu.VMEM((HEADS, 2 * HEAD_DIM, PATCH), bf16),
         heads=pltpu.VMEM((C, PATCH), f32),
         live=pltpu.VMEM((PATCH, C), f32),
-        bd=pltpu.VMEM((PATCH // QB, QB, QB), f32),
+        own=pltpu.VMEM((HEADS, 1, PATCH), f32),
         sbuf=pltpu.VMEM((2, PATCH, QB), f32),
         starts=pltpu.SMEM((devices,), jnp.int32),
         rowbuf=pltpu.VMEM((2, per * cap, C), f32),

time: 91.4 us -> 91.2 us (level)
  no operation moved by 1% of the time
where the time goes in v6:
time: 91.2 us; the launch traced here: 91 us
  Pallas kernels  88.6 us (97%)
  local copies, waits for them, and re-layouts  2.46 us (3%)
    pallas_call x1, Pallas kernels, body(): pl.pallas_call(functools.partial(block_kernel, cap, per, names), out_shap...  88.6 us
    unnamed x1, local copies, waits for them, and re-layouts  2.46 us

profile of v6, /device:TPU:1, one launch (start us, length us, event | category | flops | bytes accessed | tf_op | source)
XLA Modules:
  0.0 91.0 jit_solution(415738781036514345)
XLA Ops:
  0.0 88.6 %block.1 = bf16[128,40,128]{2,1,0:T(8,128)(2,1)} custom-call(bf16[16,16,16,128]{3,2,1,0:T(8,128)(2,1)} %bitcast.7, s32[1,4096]{1,0:T(1,128)} %bitcast.8, s32[1,4096]{1,0:T(1,128)} %refs_2_.1, s32[1,4096]{1,0:T(1,128)} %refs_3_.1, s32[1,4096]{1,0:T(1,128)} %refs_4_.1, s32[1,128]{1,0:T(1,128)} %refs_5_.1, bf16[27,128,128]{2,1,0:T(8,128)(2,1)} %refs_6_.1, ...), custom_call_target="tpu_custom_call" | custom-call | tf_op jit(solution)/shard_map/block/pallas_call | solution.py:514
  88.6 2.5 %copy.17 = bf16[5120,128]{1,0:T(8,128)(2,1)} copy(bf16[5120,128]{1,0:T(8,128)(2,1)} %bitcast.6) | data formatting | bytes 2621440

commit v7 on v6

--- a/solution.py
+++ b/solution.py
@@ -92,7 +92,7 @@
 
 def encode(r, wait_for):
     pts, occ, wconv, proj, cgain = r.pts, r.occ, r.wconv, r.proj, r.cgain
-    residual, win, taps = r.residual, r.win, r.taps
+    residual, win, taps, early = r.residual, r.win, r.taps, r.early
     halo_send, halo_recv, side_sem = r.halo_send, r.halo_recv, r.side_sem
     n_x, n_y = lax.axis_size("gx"), lax.axis_size("gy")
     me_x, me_y = lax.axis_index("gx"), lax.axis_index("gy")
@@ -152,6 +152,14 @@
                 device_id_type=pl.DeviceIdType.MESH,
             )
         )
+
+    def shift(r, carry):
+        a, b, row, block = own_block(r)
+        for dz in (-1, 1):
+            put(dz, a + 1, pl.ds(b + 1, cols), jnp.dot(pick(dz, row), block, preferred_element_type=jnp.float32))
+        return carry
+
+    lax.fori_loop(0, LA * LB // cols, shift, 0, unroll=4)
     wait_for("order", "cnt")
     offsets(r)
     pl.semaphore_wait(barrier, len(met))
@@ -160,13 +168,6 @@
     for device in col:
         pl.semaphore_signal(side_sem, inc=1, device_id=device, device_id_type=pl.DeviceIdType.MESH)
 
-    def shift(r, carry):
-        a, b, row, block = own_block(r)
-        for dz in (-1, 1):
-            put(dz, a + 1, pl.ds(b + 1, cols), jnp.dot(pick(dz, row), block, preferred_element_type=jnp.float32))
-        return carry
-
-    lax.fori_loop(0, LA * LB // cols, shift, 0, unroll=4)
     wait_for("wconv", "proj", "cgain")
     prepare(r)
 
@@ -178,6 +179,35 @@
                 taps[at : at + C, :C] = wconv[i * 9 + sb * 3 + sz] if i < 3 else none
                 taps[at : at + C, C:] = wconv[(i - 1) * 9 + sb * 3 + sz] if i > 0 else none
 
+    tall = 2
+    wide = LB * z
+    inner = range(1, LA // 2 // tall - 1)
+
+    def products(t, sb):
+        total = None
+        for pair in range(2):
+            pieces = []
+            for i in (2 * pair, 2 * pair + 1):
+                for sz in range(3):
+                    pieces.append(
+                        jnp.concatenate(
+                            [
+                                win[sz, (t * tall + u) * 2 + i, sb : sb + LB].reshape(wide, C)
+                                for u in range(tall)
+                            ],
+                            axis=0,
+                        )
+                    )
+            w = jnp.concatenate(
+                [taps[((i * 3 + sb) * 3) * C : ((i * 3 + sb) * 3 + 3) * C, :] for i in (2 * pair, 2 * pair + 1)],
+                axis=0,
+            )
+            term = jnp.dot(jnp.concatenate(pieces, axis=1), w, preferred_element_type=jnp.float32)
+            total = term if total is None else total + term
+        return total
+
+    for t in inner:
+        early[t - 1] = products(t, 1)
     for copy in copies:
         copy.wait()
 
@@ -202,31 +232,10 @@
         for b, live_y in ((0, low_y), (LB + 1, high_y)):
             edge(a, pl.ds(b, 1), 1, live_x * live_y)
 
-    tall = 2
-    wide = LB * z
-
     def conv(t):
-        total = None
-        for sb in range(3):
-            for pair in range(2):
-                pieces = []
-                for i in (2 * pair, 2 * pair + 1):
-                    for sz in range(3):
-                        pieces.append(
-                            jnp.concatenate(
-                                [
-                                    win[sz, (t * tall + u) * 2 + i, sb : sb + LB].reshape(wide, C)
-                                    for u in range(tall)
-                                ],
-                                axis=0,
-                            )
-                        )
-                w = jnp.concatenate(
-                    [taps[((i * 3 + sb) * 3) * C : ((i * 3 + sb) * 3 + 3) * C, :] for i in (2 * pair, 2 * pair + 1)],
-                    axis=0,
-                )
-                term = jnp.dot(jnp.concatenate(pieces, axis=1), w, preferred_element_type=jnp.float32)
-                total = term if total is None else total + term
+        total = early[t - 1] if t in inner else products(t, 1)
+        total = total + products(t, 0)
+        total = total + products(t, 2)
         for o in range(2):
             conv_out = total[:, o * C : (o + 1) * C].astype(jnp.bfloat16)
             encoded = norm_rows(
@@ -371,7 +380,7 @@
     mesh_id = pl.DeviceIdType.MESH
 
     def target(c, d):
-        return me_x ^ d, me_y ^ (c ^ (d * (n_y // n_x)))
+        return (me_x + d) & (n_x - 1), me_y ^ (c ^ (d * (n_y // n_x)))
 
     wait_for("mgain", "wup", "wdown")
 
@@ -492,6 +501,7 @@
         serial=pltpu.VMEM((rows, C), f32),
         win=pltpu.VMEM((3, LA + 2, LB + 2, depth, C), bf16),
         taps=pltpu.VMEM((36 * C, 2 * C), bf16),
+        early=pltpu.VMEM((LA // 4 - 2, 2 * LB * depth, 2 * C), f32),
         qw=pltpu.VMEM((HEADS, 2 * C, PATCH), bf16),
         ka=pltpu.VMEM((2, PATCH, 2 * C), bf16),
         vt=pltpu.VMEM((HEADS, 2 * HEAD_DIM, PATCH), bf16),

time: 91.2 us -> 88.4 us (0.969)
  Pallas kernels: 88.6 us -> 85.8 us
    pallas_call x1, Pallas kernels: 88.6 us -> 85.8 us  [body(): pl.pallas_call(functools.partial(block_kernel, cap, per, names), out_shap...]
where the time goes in v7:
time: 88.4 us; the launch traced here: 88.3 us
  Pallas kernels  85.8 us (97%)
  local copies, waits for them, and re-layouts  2.46 us (3%)
    pallas_call x1, Pallas kernels, body(): pl.pallas_call(functools.partial(block_kernel, cap, per, names), out_shap...  85.8 us
    unnamed x1, local copies, waits for them, and re-layouts  2.46 us

profile of v7, /device:TPU:1, one launch (start us, length us, event | category | flops | bytes accessed | tf_op | source)
XLA Modules:
  0.0 88.3 jit_solution(5743015676421951167)
XLA Ops:
  0.0 85.8 %block.1 = bf16[128,40,128]{2,1,0:T(8,128)(2,1)} custom-call(bf16[16,16,16,128]{3,2,1,0:T(8,128)(2,1)} %bitcast.7, s32[1,4096]{1,0:T(1,128)} %bitcast.8, s32[1,4096]{1,0:T(1,128)} %refs_2_.1, s32[1,4096]{1,0:T(1,128)} %refs_3_.1, s32[1,4096]{1,0:T(1,128)} %refs_4_.1, s32[1,128]{1,0:T(1,128)} %refs_5_.1, bf16[27,128,128]{2,1,0:T(8,128)(2,1)} %refs_6_.1, ...), custom_call_target="tpu_custom_call" | custom-call | tf_op jit(solution)/shard_map/block/pallas_call | solution.py:524
  85.8 2.5 %copy.17 = bf16[5120,128]{1,0:T(8,128)(2,1)} copy(bf16[5120,128]{1,0:T(8,128)(2,1)} %bitcast.6) | data formatting | bytes 2621440

commit v8 on v7

--- a/solution.py
+++ b/solution.py
@@ -16,7 +16,7 @@
 HEAD_DIM = 16
 QB = 256
 KB = 512
-UNROLL = 2
+UNROLL = 4
 
 
 def norm_rows(v, gain):
@@ -181,11 +181,12 @@
 
     tall = 2
     wide = LB * z
-    inner = range(1, LA // 2 // tall - 1)
-
-    def products(t, sb):
+    steps = LA // 2 // tall
+    edges = {0: (1,), steps - 1: (0,)}
+
+    def products(t, sb, pairs=(0, 1)):
         total = None
-        for pair in range(2):
+        for pair in pairs:
             pieces = []
             for i in (2 * pair, 2 * pair + 1):
                 for sz in range(3):
@@ -206,8 +207,8 @@
             total = term if total is None else total + term
         return total
 
-    for t in inner:
-        early[t - 1] = products(t, 1)
+    for t in range(steps):
+        early[t] = products(t, 1, edges.get(t, (0, 1)))
     for copy in copies:
         copy.wait()
 
@@ -233,8 +234,9 @@
             edge(a, pl.ds(b, 1), 1, live_x * live_y)
 
     def conv(t):
-        total = early[t - 1] if t in inner else products(t, 1)
-        total = total + products(t, 0)
+        total = early[t] + products(t, 0)
+        if t in edges:
+            total = total + products(t, 1, (1 - edges[t][0],))
         total = total + products(t, 2)
         for o in range(2):
             conv_out = total[:, o * C : (o + 1) * C].astype(jnp.bfloat16)
@@ -247,7 +249,7 @@
                     pts[a].reshape(wide, C).astype(jnp.float32) + encoded[u * wide : (u + 1) * wide]
                 )
 
-    for t in range(LA // 2 // tall):
+    for t in range(steps):
         conv(t)
 
 
@@ -501,7 +503,7 @@
         serial=pltpu.VMEM((rows, C), f32),
         win=pltpu.VMEM((3, LA + 2, LB + 2, depth, C), bf16),
         taps=pltpu.VMEM((36 * C, 2 * C), bf16),
-        early=pltpu.VMEM((LA // 4 - 2, 2 * LB * depth, 2 * C), f32),
+        early=pltpu.VMEM((LA // 4, 2 * LB * depth, 2 * C), f32),
         qw=pltpu.VMEM((HEADS, 2 * C, PATCH), bf16),
         ka=pltpu.VMEM((2, PATCH, 2 * C), bf16),
         vt=pltpu.VMEM((HEADS, 2 * HEAD_DIM, PATCH), bf16),

time: 88.4 us -> 84.1 us (0.951)
  Pallas kernels: 85.8 us -> 81.5 us
    pallas_call x1, Pallas kernels: 85.8 us -> 81.5 us  [body(): pl.pallas_call(functools.partial(block_kernel, cap, per, names), out_shap...]
where the time goes in v8:
time: 84.1 us; the launch traced here: 83.9 us
  Pallas kernels  81.5 us (97%)
  local copies, waits for them, and re-layouts  2.46 us (3%)
    pallas_call x1, Pallas kernels, body(): pl.pallas_call(functools.partial(block_kernel, cap, per, names), out_shap...  81.5 us
    unnamed x1, local copies, waits for them, and re-layouts  2.46 us

profile of v8, /device:TPU:1, one launch (start us, length us, event | category | flops | bytes accessed | tf_op | source)
XLA Modules:
  0.0 83.9 jit_solution(8279073667351346104)
XLA Ops:
  0.0 81.5 %block.1 = bf16[128,40,128]{2,1,0:T(8,128)(2,1)} custom-call(bf16[16,16,16,128]{3,2,1,0:T(8,128)(2,1)} %bitcast.7, s32[1,4096]{1,0:T(1,128)} %bitcast.8, s32[1,4096]{1,0:T(1,128)} %refs_2_.1, s32[1,4096]{1,0:T(1,128)} %refs_3_.1, s32[1,4096]{1,0:T(1,128)} %refs_4_.1, s32[1,128]{1,0:T(1,128)} %refs_5_.1, bf16[27,128,128]{2,1,0:T(8,128)(2,1)} %refs_6_.1, ...), custom_call_target="tpu_custom_call" | custom-call | tf_op jit(solution)/shard_map/block/pallas_call | solution.py:526
  81.5 2.5 %copy.17 = bf16[5120,128]{1,0:T(8,128)(2,1)} copy(bf16[5120,128]{1,0:T(8,128)(2,1)} %bitcast.6) | data formatting | bytes 2621440
